TPU v7x, 512 devices: a whole 4x8x8 slice. The times are simulated.
512 devices in a mesh: sec: 2 (over x_lo), gx: 128 (over y, z, core), gy: 2 (over x_hi).
Axes of the slice: x: 4 (x_hi: 2, x_lo: 2; x = x_hi * 2 + x_lo), y: 8, z: 8, core: 2. Of those that a mesh axis runs over, the one named last changes fastest.
Arguments:
- sections: float32 [2, 8, 2048, 64, 128], P('sec', None, 'gx', 'gy'), may hold values from -4 to 8, as said below
- fiber_angles: float32 [8, 2], replicated, may hold values from -3.140625 to 3.140625
- fiber_class: int32 [2048, 64, 8], P('gx', 'gy'), may hold values from 0 to 7
- row_map: int32 [128, 2, 512], P('gx', 'gy'), may hold values from 0 to 511, each once within a row
- interface_rows: int32 [2, 128, 2, 32], P(None, 'gx', 'gy'), may hold values from 0 to 31, each once within a row
Outputs:
- updated: float32 [2, 4, 2048, 64, 128], P('sec', None, 'gx', 'gy')
Inputs may be any that keep to these rules, and one draw needn't show every extreme that they name: sections[0] holds calcium of 0.05 to 1, gates of 0 to 1, a bound buffer of 0 to 0.8 and tension of 0 to 1; sections[1] holds a stiffness of 0.5 to 2 and an activation coefficient of 2 to 8. `fiber_class`: the class of each column's block of 16 cells through the thickness. `row_map`: each block's list is a permutation of its 512 column places. `interface_rows`: for each side and block, a permutation of the 32 rows.
All inputs are finite; a program needn't handle non-finite values.
Results may differ from a plain program's by a relative error of at most 0.00002.
Values sent between devices are 32-bit elements; how exact they have to be, the bound alone decides.
A program may use at most 64 MiB of HBM per device.

v0:
```python
import jax
import jax.numpy as jnp
from jax import lax
from jax.sharding import PartitionSpec as P

STEPS = 2
SWEEPS = 2


sigma_long = 1.0
sigma_cross = 0.25
time_step = 0.1
shear_modulus = 1.0
lame_first = 1.0
relax_weight = 0.6
tie_stiffness = 2.0
diagonal_coef = 10.0


def extended_2(block, sides, width):
    for axis, dim in sides:
        count = lax.axis_size(axis)
        forward = [(i, i + 1) for i in range(count - 1)]
        forward.append((count - 1, 0))
        backward = [(target, source) for source, target in forward]
        low = lax.ppermute(
            lax.slice_in_dim(block, block.shape[dim] - width, None, axis=dim), axis, forward
        )
        high = lax.ppermute(lax.slice_in_dim(block, 0, width, axis=dim), axis, backward)
        block = jnp.concatenate([low, block, high], axis=dim)
    return block


def from_behind(block, axis, distance):
    devices = range(lax.axis_size(axis))
    route = [(i - distance, i) for i in devices if i - distance in devices]
    return lax.ppermute(block, axis, route)


def fiber_table(fiber_angles):
    azimuth = fiber_angles[:, 0]
    elevation = fiber_angles[:, 1]
    fiber_dir = [
        jnp.cos(azimuth) * jnp.cos(elevation),
        jnp.sin(azimuth) * jnp.cos(elevation),
        jnp.sin(elevation),
    ]
    spread_gap = sigma_long - sigma_cross
    return jnp.stack(
        fiber_dir
        + [
            sigma_cross + spread_gap * fiber_dir[0] * fiber_dir[0],
            sigma_cross + spread_gap * fiber_dir[1] * fiber_dir[1],
            sigma_cross + spread_gap * fiber_dir[2] * fiber_dir[2],
            spread_gap * fiber_dir[0] * fiber_dir[1],
            spread_gap * fiber_dir[0] * fiber_dir[2],
            spread_gap * fiber_dir[1] * fiber_dir[2],
        ]
    )


def cell_values(fiber_class, fiber_rows, block_depth):
    class_count = fiber_rows.shape[1]
    onehot = (fiber_class[..., None] == jnp.arange(class_count, dtype=jnp.int32)).astype(
        jnp.float32
    )
    picked = jnp.sum(onehot[None] * fiber_rows[:, None, None, None, :], axis=-1)
    widened = jnp.broadcast_to(picked[..., None], picked.shape + (block_depth,))
    return widened.reshape(picked.shape[:-1] + (picked.shape[-1] * block_depth,))


def window(values, offset):
    size_x = values.shape[-3] - 2
    size_y = values.shape[-2] - 2
    size_z = values.shape[-1] - 2
    return values[
        ...,
        1 + offset[0] : 1 + offset[0] + size_x,
        1 + offset[1] : 1 + offset[1] + size_y,
        1 + offset[2] : 1 + offset[2] + size_z,
    ]


def unit_vec(axis_a, factor):
    return tuple((factor if place_a == axis_a else 0 for place_a in range(3)))


def add_offsets(first_off, second_off):
    return tuple((first_off[place_a] + second_off[place_a] for place_a in range(3)))


def second_diff(pick_cells, values, axis_a, centre):
    return (
        pick_cells(values, unit_vec(axis_a, 1))
        - 2.0 * centre
        + pick_cells(values, unit_vec(axis_a, -1))
    )


def cross_diff(pick_cells, values, axis_a, axis_b):
    plus_a, minus_a = (unit_vec(axis_a, 1), unit_vec(axis_a, -1))
    plus_b, minus_b = (unit_vec(axis_b, 1), unit_vec(axis_b, -1))
    return 0.25 * (
        pick_cells(values, add_offsets(plus_a, plus_b))
        - pick_cells(values, add_offsets(plus_a, minus_b))
        - pick_cells(values, add_offsets(minus_a, plus_b))
        + pick_cells(values, add_offsets(minus_a, minus_b))
    )


def diffuse(pick_cells, values, cell_fiber):
    centre = pick_cells(values, (0, 0, 0))
    result = jnp.zeros_like(centre)
    for axis_a in range(3):
        result = result + cell_fiber[3 + axis_a] * second_diff(pick_cells, values, axis_a, centre)
    for pair_axes, slot_index in (((0, 1), 6), ((0, 2), 7), ((1, 2), 8)):
        result = result + 2.0 * cell_fiber[slot_index] * cross_diff(
            pick_cells, values, pair_axes[0], pair_axes[1]
        )
    return result


def ionic_step(cell_state, diffusion):
    voltage, calcium, activation, inactivation, potassium, slow_gate, buffered, tension = cell_state
    bound_share = calcium * calcium / (calcium * calcium + 0.25)
    calcium_flow = 1.2 * activation * inactivation * (voltage - 2.0)
    current_sum = (
        calcium_flow
        + 0.8 * potassium * (voltage + 1.0)
        + 0.6 * bound_share * slow_gate * (voltage + 1.0)
        + 0.1 * voltage
    )
    binding = 2.0 * calcium * (1.0 - buffered) - 0.4 * buffered
    return [
        voltage + time_step * (diffusion - current_sum),
        calcium + time_step * (-0.3 * calcium_flow - 0.5 * calcium - binding),
        activation + time_step * (jax.nn.sigmoid(2.0 * voltage + 1.0) - activation) / 0.5,
        inactivation + time_step * (jax.nn.sigmoid(-2.0 * voltage) - inactivation) / 3.0,
        potassium + time_step * (jax.nn.sigmoid(2.0 * voltage) - potassium),
        slow_gate + time_step * (jax.nn.sigmoid(voltage - 0.5) - slow_gate) / 5.0,
        buffered + time_step * binding,
        tension + time_step * (bound_share - tension) / 2.0,
    ]


def navier(pick_cells, motion, stiffness):
    centre = pick_cells(motion, (0, 0, 0))
    laplace = jnp.zeros_like(centre)
    for axis_a in range(3):
        laplace = laplace + second_diff(pick_cells, motion, axis_a, centre)
    pieces = []
    for component in range(3):
        component_term = second_diff(pick_cells, motion[component], component, centre[component])
        for other_axis in range(3):
            if other_axis != component:
                component_term = component_term + cross_diff(
                    pick_cells, motion[other_axis], component, other_axis
                )
        pieces.append(component_term)
    graddiv = jnp.stack(pieces)
    return (centre, -stiffness * (shear_modulus * laplace + (lame_first + shear_modulus) * graddiv))


def tie_forces(partial_value, from_left, from_right, rows_first, rows_last):
    left_term = jnp.take(from_left, rows_first, axis=1) - partial_value[:, 0]
    right_term = jnp.take(from_right, rows_last, axis=1) - partial_value[:, -1]
    return jnp.zeros_like(partial_value).at[:, 0].add(left_term).at[:, -1].add(right_term)


def relax_sweep(motion, stiffness, drive, rows_first, rows_last):
    partial_value = tie_stiffness * stiffness * motion
    extended = extended_2(motion, (("gx", 1), ("gy", 2)), 1)
    face_pairs = jnp.stack([partial_value[:, 0], partial_value[:, -1]], axis=1)
    received_faces = extended_2(face_pairs, (("gx", 1),), 1)
    from_left = received_faces[:, 0]
    from_right = received_faces[:, 3]
    extended = jnp.pad(extended, ((0, 0), (0, 0), (0, 0), (1, 1)))
    centre, applied = navier(window, extended, stiffness)
    tie_force = tie_forces(partial_value, from_left, from_right, rows_first, rows_last)
    return centre + relax_weight * (drive + tie_force - applied) / (diagonal_coef * stiffness)


def local(sections, fiber_angles, fiber_class, row_map, interface_rows):
    own_data = sections[0]
    fiber_rows = fiber_table(fiber_angles)
    cell_fiber = cell_values(fiber_class, fiber_rows, own_data.shape[-1] // fiber_class.shape[-1])
    cell_state = [own_data[channel] for channel in range(8)]
    for repeat in range(STEPS):
        extended = extended_2(cell_state[0], (("gx", 0), ("gy", 1)), 1)
        extended = jnp.pad(extended, ((0, 0), (0, 0), (1, 1)))
        diffusion = diffuse(window, extended, cell_fiber)
        cell_state = ionic_step(cell_state, diffusion)
    tension_out = cell_state[7]
    received = from_behind(tension_out, "sec", 1)
    slab_shape = received.shape
    remapped = jnp.take(
        received.reshape(slab_shape[0] * slab_shape[1], slab_shape[2]), row_map[0, 0], axis=0
    )
    activity = own_data[7] * remapped.reshape(slab_shape)
    motion = own_data[0:3]
    stiffness = own_data[6]
    drive = own_data[3:6] + activity * cell_fiber[0:3]
    rows_first = interface_rows[0, 0, 0]
    rows_last = interface_rows[1, 0, 0]
    for repeat in range(SWEEPS):
        motion = relax_sweep(motion, stiffness, drive, rows_first, rows_last)
    electric_out = jnp.stack([cell_state[0], cell_state[1], cell_state[4], cell_state[7]])
    mechanic_out = jnp.concatenate([motion, activity[None]], axis=0)
    sec_place = lax.axis_index("sec")
    return jnp.where(sec_place == 0, electric_out, mechanic_out)[None]


def solution(mesh):
    in_specs = (
        P("sec", None, "gx", "gy", None),
        P(),
        P("gx", "gy", None),
        P("gx", "gy", None),
        P(None, "gx", "gy", None),
    )
    out_specs = P("sec", None, "gx", "gy", None)
    return jax.shard_map(local, mesh=mesh, in_specs=in_specs, out_specs=out_specs, check_vma=False)
```

profile of v0, /device:TPU:1, one launch (start us, length us, event | category | flops | bytes accessed | tf_op | source)
XLA Modules:
  0.0 171.8 jit_solution(3151517379566849042)
XLA Ops:
  0.0 1.4 slice_bitcast_fusion.12
  1.4 5.4 %collective-permute-start.1 = (f32[1,32,128]{2,1,0:T(8,128)}, f32[1,32,128]{2,1,0:T(8,128)}, u32[]{:S(2)}, u32[]{:S(2)}) collective-permute-start(f32[1,32,128]{2,1,0:T(8,128)} %get-tuple-element.86), channel_id=1, source_target_pairs={{0,2},{2,4},{4,6},{6,8},{8,10},{10,12},{12,14},{14,16},{16,18},{18... | collective-permute-start | bytes 49160 | tf_op jit(solution)/shard_map/ppermute | solution.py:26
  6.8 5.3 %collective-permute-start = (f32[1,32,128]{2,1,0:T(8,128)}, f32[1,32,128]{2,1,0:T(8,128)}, u32[]{:S(2)}, u32[]{:S(2)}) collective-permute-start(f32[1,32,128]{2,1,0:T(8,128)} %get-tuple-element.87), channel_id=1, source_target_pairs={{2,0},{4,2},{6,4},{8,6},{10,8},{12,10},{14,12},{16,14},{18,16},{20... | collective-permute-start | bytes 49160 | tf_op jit(solution)/shard_map/ppermute | solution.py:29
  12.1 2.5 %fusion.158 = (f32[1,3,16,32,128]{4,3,2,1,0:T(8,128)}, f32[3,16,32,128]{3,2,1,0:T(8,128)S(1)}) fusion(f32[1,8,16,32,128]{4,3,2,1,0:T(8,128)} %param.15), kind=kLoop, calls=%fused_computation.386 | loop fusion | bytes 3145728 | tf_op jit(solution)/shard_map/slice | solution.py:202
  14.6 1.9 %collective-permute-start.12 = (f32[3,1,32,128]{3,2,1,0:T(8,128)S(1)}, f32[3,1,32,128]{3,2,1,0:T(8,128)S(1)}, u32[]{:S(2)}, u32[]{:S(2)}) collective-permute-start(f32[3,1,32,128]{3,2,1,0:T(8,128)S(1)} %get-tuple-element.98), channel_id=1, source_target_pairs={{0,2},{2,4},{4,6},{6,8},{8,10},{10,12},{12,14},{14,16},{16,18},{18... | collective-permute-start | bytes 147464 | tf_op jit(solution)/shard_map/ppermute | solution.py:26
  16.5 7.9 %collective-permute-start.11 = (f32[3,1,32,128]{3,2,1,0:T(8,128)S(1)}, f32[3,1,32,128]{3,2,1,0:T(8,128)S(1)}, u32[]{:S(2)}, u32[]{:S(2)}) collective-permute-start(f32[3,1,32,128]{3,2,1,0:T(8,128)S(1)} %get-tuple-element.99), channel_id=1, source_target_pairs={{2,0},{4,2},{6,4},{8,6},{10,8},{12,10},{14,12},{16,14},{18,16},{20... | collective-permute-start | bytes 147464 | tf_op jit(solution)/shard_map/ppermute | solution.py:29
  25.3 1.4 multiply_reduce_fusion
  26.8 0.8 slice_bitcast_fusion.10
  28.2 4.7 %collective-permute-start.14 = (f32[3,18,1,128]{3,2,1,0:T(1,128)S(1)}, f32[3,18,1,128]{3,2,1,0:T(1,128)S(1)}, u32[]{:S(2)}, u32[]{:S(2)}) collective-permute-start(f32[3,18,1,128]{3,2,1,0:T(1,128)S(1)} %get-tuple-element.90), channel_id=1, source_target_pairs={{0,1},{1,0},{2,3},{3,2},{4,5},{5,4},{6,7},{7,6},{8,9},{9,8},{10,11... | collective-permute-start | bytes 82952 | tf_op jit(solution)/shard_map/ppermute | solution.py:26
  32.9 2.1 %collective-permute-start.13 = (f32[3,18,1,128]{3,2,1,0:T(1,128)S(1)}, f32[3,18,1,128]{3,2,1,0:T(1,128)S(1)}, u32[]{:S(2)}, u32[]{:S(2)}) collective-permute-start(f32[3,18,1,128]{3,2,1,0:T(1,128)S(1)} %get-tuple-element.91), channel_id=1, source_target_pairs={{1,0},{0,1},{3,2},{2,3},{5,4},{4,5},{7,6},{6,7},{9,8},{8,9},{11,10... | collective-permute-start | bytes 82952 | tf_op jit(solution)/shard_map/ppermute | solution.py:29
  35.6 3.4 %collective-permute-done.13 = f32[3,18,1,128]{3,2,1,0:T(1,128)S(1)} collective-permute-done((f32[3,18,1,128]{3,2,1,0:T(1,128)S(1)}, f32[3,18,1,128]{3,2,1,0:T(1,128)S(1)}, u32[]{:S(2)}, u32[]{:S(2)}) %collective-permute-start.13) | collective-permute-done | bytes 27680 | tf_op jit(solution)/shard_map/ppermute | solution.py:29
  39.0 0.9 select_maximum_fusion.4
  40.1 1.2 copy-done.1
  41.3 1.5 copy-done
  42.9 1.6 bitcast_negate_fusion
  44.5 2.2 %collective-permute-start.8 = (f32[16,32,128]{2,1,0:T(8,128)}, f32[16,32,128]{2,1,0:T(8,128)S(1)}, u32[]{:S(2)}, u32[]{:S(2)}) collective-permute-start(f32[16,32,128]{2,1,0:T(8,128)} %get-tuple-element.74), channel_id=1, source_target_pairs={{0,256},{1,257},{2,258},{3,259},{4,260},{5,261},{6,262},{7,263},{8... | collective-permute-start | bytes 786440 | tf_op jit(solution)/shard_map/ppermute | solution.py:37
  49.2 1.0 broadcast_in_dim.60
  50.2 1.5 copy.153
  51.7 1.1 broadcast_in_dim.68
  52.8 2.2 %copy.158 = f32[16,32,128]{2,1,0:T(8,128)} copy(f32[16,32,128]{1,2,0:T(8,128)} %bitcast.320) | data formatting | bytes 524288 | tf_op jit(solution)/shard_map/mul | solution.py:117
  55.0 1.0 broadcast_in_dim.67
  56.1 2.2 %copy.157 = f32[16,32,128]{2,1,0:T(8,128)} copy(f32[16,32,128]{1,2,0:T(8,128)} %bitcast.321) | data formatting | bytes 524288 | tf_op jit(solution)/shard_map/mul | solution.py:117
  58.3 1.0 broadcast_in_dim.66
  59.3 2.2 %copy.156 = f32[16,32,128]{2,1,0:T(8,128)} copy(f32[16,32,128]{1,2,0:T(8,128)} %bitcast.322) | data formatting | bytes 524288 | tf_op jit(solution)/shard_map/mul | solution.py:117
  61.6 1.9 %broadcast_in_dim.64 = f32[16,32,8,16]{1,3,2,0:T(8,128)} broadcast(f32[16,32,8]{1,2,0:T(8,128)} %get-tuple-element.104), dimensions={0,1,2} | broadcast | bytes 278528 | tf_op jit(solution)/shard_map/broadcast_in_dim | solution.py:68
  63.5 2.3 %copy.155 = f32[16,32,128]{2,1,0:T(8,128)} copy(f32[16,32,128]{1,2,0:T(8,128)} %bitcast.323) | data formatting | bytes 524288 | tf_op jit(solution)/shard_map/broadcast_in_dim | solution.py:68
  65.8 1.9 %broadcast_in_dim.62 = f32[16,32,8,16]{1,3,2,0:T(8,128)} broadcast(f32[16,32,8]{1,2,0:T(8,128)} %get-tuple-element.105), dimensions={0,1,2} | broadcast | bytes 278528 | tf_op jit(solution)/shard_map/broadcast_in_dim | solution.py:68
  67.7 2.3 %copy.154 = f32[16,32,128]{2,1,0:T(8,128)} copy(f32[16,32,128]{1,2,0:T(8,128)} %bitcast.324) | data formatting | bytes 524288 | tf_op jit(solution)/shard_map/broadcast_in_dim | solution.py:68
  69.9 1.9 %broadcast_in_dim.71 = f32[3,16,32,8,16]{2,4,3,1,0:T(8,128)} broadcast(f32[3,16,32,8]{2,3,1,0:T(8,128)S(1)} %slice-done), dimensions={0,1,2,3} | broadcast | bytes 835584 | tf_op jit(solution)/shard_map/broadcast_in_dim | solution.py:68
  71.8 3.1 %copy.166 = f32[3,16,32,128]{3,2,0,1:T(8,128)} copy(f32[3,16,32,128]{2,3,1,0:T(8,128)} %bitcast.318) | data formatting | bytes 1572864 | tf_op jit(solution)/shard_map/slice | solution.py:202
  75.0 1.6 gather_fusion
  76.6 2.1 %select_multiply_fusion = (f32[1,1,16,32,128]{4,3,2,1,0:T(8,128)}, f32[1,1,16,32,128]{4,3,2,1,0:T(8,128)}, f32[16,32,128]{2,1,0:T(8,128)S(1)}) fusion(f32[1,1,16,32,128]{4,3,2,1,0:T(8,128)} %bitcast.325, f32[1,8,16,32,128]{4,3,2,1,0:T(8,128)S(1)} %copy-done, pred[16,32]{1,0:T(8,128)(4,1)S(1)} %compare_and_fusion), kind=kLoop, calls=%fused_computation.320 | loop fusion | flops 1900544 | bytes 2621952 | tf_op jit(solution)/shard_map/mul | solution.py:199
  79.5 3.6 %collective-permute-start.3 = (f32[18,1,128]{2,1,0:T(1,128)S(1)}, f32[18,1,128]{2,1,0:T(1,128)S(1)}, u32[]{:S(2)}, u32[]{:S(2)}) collective-permute-start(f32[18,1,128]{2,1,0:T(1,128)S(1)} %get-tuple-element.112), channel_id=1, source_target_pairs={{0,1},{1,0},{2,3},{3,2},{4,5},{5,4},{6,7},{7,6},{8,9},{9,8},{10,11... | collective-permute-start | bytes 27656 | tf_op jit(solution)/shard_map/ppermute | solution.py:26
  83.2 3.3 %collective-permute-start.2 = (f32[18,1,128]{2,1,0:T(1,128)S(1)}, f32[18,1,128]{2,1,0:T(1,128)S(1)}, u32[]{:S(2)}, u32[]{:S(2)}) collective-permute-start(f32[18,1,128]{2,1,0:T(1,128)S(1)} %get-tuple-element.113), channel_id=1, source_target_pairs={{1,0},{0,1},{3,2},{2,3},{5,4},{4,5},{7,6},{6,7},{9,8},{8,9},{11,10... | collective-permute-start | bytes 27656 | tf_op jit(solution)/shard_map/ppermute | solution.py:29
  86.5 1.2 fusion.56
  87.7 1.5 collective-permute-done.2
  89.2 1.1 select_maximum_fusion.12
  90.3 0.9 pad_maximum_fusion.16
  91.2 2.5 %add_bitcast_fusion = (f32[1,1,16,32,128]{4,3,2,1,0:T(8,128)}, f32[16,32,128]{2,1,0:T(8,128)S(1)}) fusion(f32[16,32,128]{2,1,0:T(8,128)S(1)} %copy-done.23, f32[1,8,16,32,128]{4,3,2,1,0:T(8,128)S(1)} %copy-done, f32[16,32,128]{2,1,0:T(8,128)S(1)} %get-tuple-element.85, f32[16,32,128]{2,1,0:T(8,128)S(1)} %copy-done.12, ...), kind=kLoop, calls=%fused_computation.322 | loop fusion | flops 5832704 | bytes 8683520 | tf_op jit(solution)/shard_map/stack | solution.py:207
  93.7 1.5 bitcast_multiply_fusion
  95.2 1.9 %collective-permute-start.5 = (f32[1,32,128]{2,1,0:T(8,128)S(1)}, f32[1,32,128]{2,1,0:T(8,128)S(1)}, u32[]{:S(2)}, u32[]{:S(2)}) collective-permute-start(f32[1,32,128]{2,1,0:T(8,128)S(1)} %get-tuple-element.114), channel_id=1, source_target_pairs={{0,2},{2,4},{4,6},{6,8},{8,10},{10,12},{12,14},{14,16},{16,18},{18... | collective-permute-start | bytes 49160 | tf_op jit(solution)/shard_map/ppermute | solution.py:26
  97.1 10.1 %collective-permute-start.4 = (f32[1,32,128]{2,1,0:T(8,128)S(1)}, f32[1,32,128]{2,1,0:T(8,128)S(1)}, u32[]{:S(2)}, u32[]{:S(2)}) collective-permute-start(f32[1,32,128]{2,1,0:T(8,128)S(1)} %get-tuple-element.115), channel_id=1, source_target_pairs={{2,0},{4,2},{6,4},{8,6},{10,8},{12,10},{14,12},{16,14},{18,16},{20... | collective-permute-start | bytes 49160 | tf_op jit(solution)/shard_map/ppermute | solution.py:29
  108.1 3.1 %collective-permute-start.7 = (f32[18,1,128]{2,1,0:T(1,128)S(1)}, f32[18,1,128]{2,1,0:T(1,128)S(1)}, u32[]{:S(2)}, u32[]{:S(2)}) collective-permute-start(f32[18,1,128]{2,1,0:T(1,128)S(1)} %get-tuple-element.108), channel_id=1, source_target_pairs={{0,1},{1,0},{2,3},{3,2},{4,5},{5,4},{6,7},{7,6},{8,9},{9,8},{10,11... | collective-permute-start | bytes 27656 | tf_op jit(solution)/shard_map/ppermute | solution.py:26
  111.2 3.6 %collective-permute-start.6 = (f32[18,1,128]{2,1,0:T(1,128)S(1)}, f32[18,1,128]{2,1,0:T(1,128)S(1)}, u32[]{:S(2)}, u32[]{:S(2)}) collective-permute-start(f32[18,1,128]{2,1,0:T(1,128)S(1)} %get-tuple-element.109), channel_id=1, source_target_pairs={{1,0},{0,1},{3,2},{2,3},{5,4},{4,5},{7,6},{6,7},{9,8},{8,9},{11,10... | collective-permute-start | bytes 27656 | tf_op jit(solution)/shard_map/ppermute | solution.py:29
  114.9 8.1 %collective-permute-start.10 = (f32[3,1,32,128]{3,2,1,0:T(8,128)S(1)}, f32[3,1,32,128]{3,2,1,0:T(8,128)S(1)}, u32[]{:S(2)}, u32[]{:S(2)}) collective-permute-start(f32[3,1,32,128]{3,2,1,0:T(8,128)S(1)} %get-tuple-element.96), channel_id=1, source_target_pairs={{2,0},{4,2},{6,4},{8,6},{10,8},{12,10},{14,12},{16,14},{18,16},{20... | collective-permute-start | bytes 147464 | tf_op jit(solution)/shard_map/ppermute | solution.py:29
  123.0 2.1 %collective-permute-start.9 = (f32[3,1,32,128]{3,2,0,1:T(8,128)S(1)}, f32[3,1,32,128]{3,2,0,1:T(8,128)S(1)}, u32[]{:S(2)}, u32[]{:S(2)}) collective-permute-start(f32[3,1,32,128]{3,2,0,1:T(8,128)S(1)} %get-tuple-element.97), channel_id=1, source_target_pairs={{0,2},{2,4},{4,6},{6,8},{8,10},{10,12},{12,14},{14,16},{16,18},{18... | collective-permute-start | bytes 147464 | tf_op jit(solution)/shard_map/ppermute | solution.py:26
  125.6 1.7 fusion.75
  127.3 2.8 %collective-permute-done.9 = f32[3,1,32,128]{3,2,0,1:T(8,128)S(1)} collective-permute-done((f32[3,1,32,128]{3,2,0,1:T(8,128)S(1)}, f32[3,1,32,128]{3,2,0,1:T(8,128)S(1)}, u32[]{:S(2)}, u32[]{:S(2)}) %collective-permute-start.9) | collective-permute-done | bytes 49184 | tf_op jit(solution)/shard_map/ppermute | solution.py:26
  130.2 0.7 gather_fusion.2
  130.9 0.7 gather_fusion.1
  131.6 0.9 fusion.154
  132.6 0.9 fusion.152
  133.5 3.7 %fusion.18 = f32[3,16,32,128]{3,2,1,0:T(8,128)S(1)} fusion(f32[3,16,32,128]{3,2,1,0:T(8,128)S(1)} %copy-done.7, f32[3,18,34,130]{3,2,1,0:T(8,128)} %copy-done.1, f32[3,18,1,128]{3,2,1,0:T(1,128)S(1)} %copy-done.35, f32[3,1,32,128]{3,2,1,0:T(8,128)S(1)} %copy-done.33, f32[3,1,32,128]{3,2,1,0:T(8,128)S(1)} %copy-done.31, f32[3,18,1,128]{3,2,1,0:T(1,128)S(1)} %copy-done.37, ...), kind=kLoop, calls=%fused_computation.49 | loop fusion | flops 5701632 | bytes 7231488 | tf_op jit(solution)/shard_map/add | solution.py:180
  137.4 1.9 %collective-permute-start.18 = (f32[3,1,32,128]{3,2,1,0:T(8,128)S(1)}, f32[3,1,32,128]{3,2,1,0:T(8,128)S(1)}, u32[]{:S(2)}, u32[]{:S(2)}) collective-permute-start(f32[3,1,32,128]{3,2,1,0:T(8,128)S(1)} %get-tuple-element.94), channel_id=1, source_target_pairs={{0,2},{2,4},{4,6},{6,8},{8,10},{10,12},{12,14},{14,16},{16,18},{18... | collective-permute-start | bytes 147464 | tf_op jit(solution)/shard_map/ppermute | solution.py:26
  139.3 8.0 %collective-permute-start.17 = (f32[3,1,32,128]{3,2,1,0:T(8,128)S(1)}, f32[3,1,32,128]{3,2,1,0:T(8,128)S(1)}, u32[]{:S(2)}, u32[]{:S(2)}) collective-permute-start(f32[3,1,32,128]{3,2,1,0:T(8,128)S(1)} %get-tuple-element.95), channel_id=1, source_target_pairs={{2,0},{4,2},{6,4},{8,6},{10,8},{12,10},{14,12},{16,14},{18,16},{20... | collective-permute-start | bytes 147464 | tf_op jit(solution)/shard_map/ppermute | solution.py:29
  147.3 7.0 %collective-permute-start.16 = (f32[3,1,32,128]{3,2,0,1:T(8,128)S(1)}, f32[3,1,32,128]{3,2,0,1:T(8,128)S(1)}, u32[]{:S(2)}, u32[]{:S(2)}) collective-permute-start(f32[3,1,32,128]{3,2,0,1:T(8,128)S(1)} %get-tuple-element.92), channel_id=1, source_target_pairs={{2,0},{4,2},{6,4},{8,6},{10,8},{12,10},{14,12},{16,14},{18,16},{20... | collective-permute-start | bytes 147464 | tf_op jit(solution)/shard_map/ppermute | solution.py:29
  154.3 1.9 %collective-permute-start.15 = (f32[3,1,32,128]{3,2,0,1:T(8,128)S(1)}, f32[3,1,32,128]{3,2,0,1:T(8,128)S(1)}, u32[]{:S(2)}, u32[]{:S(2)}) collective-permute-start(f32[3,1,32,128]{3,2,0,1:T(8,128)S(1)} %get-tuple-element.93), channel_id=1, source_target_pairs={{0,2},{2,4},{4,6},{6,8},{8,10},{10,12},{12,14},{14,16},{16,18},{18... | collective-permute-start | bytes 147464 | tf_op jit(solution)/shard_map/ppermute | solution.py:26
  156.3 3.1 %collective-permute-start.20 = (f32[3,18,1,128]{3,2,1,0:T(1,128)S(1)}, f32[3,18,1,128]{3,2,1,0:T(1,128)S(1)}, u32[]{:S(2)}, u32[]{:S(2)}) collective-permute-start(f32[3,18,1,128]{3,2,1,0:T(1,128)S(1)} %get-tuple-element.88), channel_id=1, source_target_pairs={{0,1},{1,0},{2,3},{3,2},{4,5},{5,4},{6,7},{7,6},{8,9},{9,8},{10,11... | collective-permute-start | bytes 82952 | tf_op jit(solution)/shard_map/ppermute | solution.py:26
  159.5 3.6 %collective-permute-start.19 = (f32[3,18,1,128]{3,2,1,0:T(1,128)S(1)}, f32[3,18,1,128]{3,2,1,0:T(1,128)S(1)}, u32[]{:S(2)}, u32[]{:S(2)}) collective-permute-start(f32[3,18,1,128]{3,2,1,0:T(1,128)S(1)} %get-tuple-element.89), channel_id=1, source_target_pairs={{1,0},{0,1},{3,2},{2,3},{5,4},{4,5},{7,6},{6,7},{9,8},{8,9},{11,10... | collective-permute-start | bytes 82952 | tf_op jit(solution)/shard_map/ppermute | solution.py:29
  163.2 0.7 gather_fusion.4
  163.9 0.7 gather_fusion.3
  165.6 0.9 select_maximum_fusion
  169.3 1.0 fusion.24
  170.6 1.2 maximum_select_fusion
  (150 shorter events, 11.1 us)
Async XLA Ops:
  0.0 24.5 %copy-start.44 = (f32[8,2]{0,1:T(2,128)S(1)}, f32[8,2]{0,1:T(2,128)}, u32[]{:S(2)}) copy-start(f32[8,2]{0,1:T(2,128)} %param.16) | copy-start | bytes 196
  0.0 24.6 %copy-start.41 = (s32[1,1,512]{2,1,0:T(1,128)S(1)}, s32[1,1,512]{2,1,0:T(1,128)}, u32[]{:S(2)}) copy-start(s32[1,1,512]{2,1,0:T(1,128)} %param.18) | copy-start | bytes 6148
  0.0 24.6 %copy-start.45 = (s32[2,1,1,32]{3,2,1,0:T(1,128)S(1)}, s32[2,1,1,32]{3,2,1,0:T(1,128)}, u32[]{:S(2)}) copy-start(s32[2,1,1,32]{3,2,1,0:T(1,128)} %param.19) | copy-start | bytes 772
  0.0 25.2 %copy-start.38 = (s32[16,32,8]{1,2,0:T(8,128)S(1)}, s32[16,32,8]{1,2,0:T(8,128)}, u32[]{:S(2)}) copy-start(s32[16,32,8]{1,2,0:T(8,128)} %param.17) | copy-start | bytes 49156
  1.4 77.3 %collective-permute-start.1 = (f32[1,32,128]{2,1,0:T(8,128)}, f32[1,32,128]{2,1,0:T(8,128)}, u32[]{:S(2)}, u32[]{:S(2)}) collective-permute-start(f32[1,32,128]{2,1,0:T(8,128)} %get-tuple-element.86), channel_id=1, source_target_pairs={{0,2},{2,4},{4,6},{6,8},{8,10},{10,12},{12,14},{14,16},{16,18},{18... | collective-permute-start | bytes 49160 | tf_op jit(solution)/shard_map/ppermute | solution.py:26
  6.8 71.9 %collective-permute-start = (f32[1,32,128]{2,1,0:T(8,128)}, f32[1,32,128]{2,1,0:T(8,128)}, u32[]{:S(2)}, u32[]{:S(2)}) collective-permute-start(f32[1,32,128]{2,1,0:T(8,128)} %get-tuple-element.87), channel_id=1, source_target_pairs={{2,0},{4,2},{6,4},{8,6},{10,8},{12,10},{14,12},{16,14},{18,16},{20... | collective-permute-start | bytes 49160 | tf_op jit(solution)/shard_map/ppermute | solution.py:29
  14.6 24.4 %copy-start.6 = (f32[3,16,32,128]{3,2,1,0:T(8,128)}, f32[3,16,32,128]{3,2,1,0:T(8,128)S(1)}, u32[]{:S(2)}) copy-start(f32[3,16,32,128]{3,2,1,0:T(8,128)S(1)} %get-tuple-element.78) | copy-start | bytes 2359300
  14.6 13.6 %collective-permute-start.12 = (f32[3,1,32,128]{3,2,1,0:T(8,128)S(1)}, f32[3,1,32,128]{3,2,1,0:T(8,128)S(1)}, u32[]{:S(2)}, u32[]{:S(2)}) collective-permute-start(f32[3,1,32,128]{3,2,1,0:T(8,128)S(1)} %get-tuple-element.98), channel_id=1, source_target_pairs={{0,2},{2,4},{4,6},{6,8},{8,10},{10,12},{12,14},{14,16},{16,18},{18... | collective-permute-start | bytes 147464 | tf_op jit(solution)/shard_map/ppermute | solution.py:26
  16.5 11.6 %collective-permute-start.11 = (f32[3,1,32,128]{3,2,1,0:T(8,128)S(1)}, f32[3,1,32,128]{3,2,1,0:T(8,128)S(1)}, u32[]{:S(2)}, u32[]{:S(2)}) collective-permute-start(f32[3,1,32,128]{3,2,1,0:T(8,128)S(1)} %get-tuple-element.99), channel_id=1, source_target_pairs={{2,0},{4,2},{6,4},{8,6},{10,8},{12,10},{14,12},{16,14},{18,16},{20... | collective-permute-start | bytes 147464 | tf_op jit(solution)/shard_map/ppermute | solution.py:29
  26.8 20.5 %copy-start.19 = (f32[9,16,32,8]{2,3,1,0:T(8,128)}, f32[9,16,32,8]{2,3,1,0:T(8,128)S(1)}, u32[]{:S(2)}) copy-start(f32[9,16,32,8]{2,3,1,0:T(8,128)S(1)} %multiply_reduce_fusion) | copy-start | bytes 442372
  28.2 10.8 %copy-start.30 = (f32[3,1,32,128]{3,2,1,0:T(8,128)}, f32[3,1,32,128]{3,2,1,0:T(8,128)S(1)}, u32[]{:S(2)}) copy-start(f32[3,1,32,128]{3,2,1,0:T(8,128)S(1)} %collective-permute-done.12) | copy-start | bytes 147460
  28.2 10.8 %copy-start.32 = (f32[3,1,32,128]{3,2,1,0:T(8,128)}, f32[3,1,32,128]{3,2,1,0:T(8,128)S(1)}, u32[]{:S(2)}) copy-start(f32[3,1,32,128]{3,2,1,0:T(8,128)S(1)} %collective-permute-done.11) | copy-start | bytes 147460
  28.2 7.4 %collective-permute-start.14 = (f32[3,18,1,128]{3,2,1,0:T(1,128)S(1)}, f32[3,18,1,128]{3,2,1,0:T(1,128)S(1)}, u32[]{:S(2)}, u32[]{:S(2)}) collective-permute-start(f32[3,18,1,128]{3,2,1,0:T(1,128)S(1)} %get-tuple-element.90), channel_id=1, source_target_pairs={{0,1},{1,0},{2,3},{3,2},{4,5},{5,4},{6,7},{7,6},{8,9},{9,8},{10,11... | collective-permute-start | bytes 82952 | tf_op jit(solution)/shard_map/ppermute | solution.py:26
  32.9 6.1 %collective-permute-start.13 = (f32[3,18,1,128]{3,2,1,0:T(1,128)S(1)}, f32[3,18,1,128]{3,2,1,0:T(1,128)S(1)}, u32[]{:S(2)}, u32[]{:S(2)}) collective-permute-start(f32[3,18,1,128]{3,2,1,0:T(1,128)S(1)} %get-tuple-element.91), channel_id=1, source_target_pairs={{1,0},{0,1},{3,2},{2,3},{5,4},{4,5},{7,6},{6,7},{9,8},{8,9},{11,10... | collective-permute-start | bytes 82952 | tf_op jit(solution)/shard_map/ppermute | solution.py:29
  35.6 4.5 %copy-start.34 = (f32[3,18,1,128]{3,2,1,0:T(1,128)}, f32[3,18,1,128]{3,2,1,0:T(1,128)S(1)}, u32[]{:S(2)}) copy-start(f32[3,18,1,128]{3,2,1,0:T(1,128)S(1)} %collective-permute-done.14) | copy-start | bytes 82948
  39.9 1.4 copy-start.1
  39.9 2.9 %copy-start = (f32[1,8,16,32,128]{4,3,2,1,0:T(8,128)S(1)}, f32[1,8,16,32,128]{4,3,2,1,0:T(8,128)}, u32[]{:S(2)}) copy-start(f32[1,8,16,32,128]{4,3,2,1,0:T(8,128)} %param.15) | copy-start | bytes 6291460
  40.1 4.4 %copy-start.2 = (f32[18,34,130]{2,1,0:T(8,128)}, f32[18,34,130]{2,1,0:T(8,128)S(1)}, u32[]{:S(2)}) copy-start(f32[18,34,130]{2,1,0:T(8,128)S(1)} %get-tuple-element.71) | copy-start | bytes 954724
  40.1 4.4 %copy-start.4 = (f32[18,34,130]{2,1,0:T(8,128)}, f32[18,34,130]{2,1,0:T(8,128)S(1)}, u32[]{:S(2)}) copy-start(f32[18,34,130]{2,1,0:T(8,128)S(1)} %get-tuple-element.69) | copy-start | bytes 954724
  44.5 30.4 %collective-permute-start.8 = (f32[16,32,128]{2,1,0:T(8,128)}, f32[16,32,128]{2,1,0:T(8,128)S(1)}, u32[]{:S(2)}, u32[]{:S(2)}) collective-permute-start(f32[16,32,128]{2,1,0:T(8,128)} %get-tuple-element.74), channel_id=1, source_target_pairs={{0,256},{1,257},{2,258},{3,259},{4,260},{5,261},{6,262},{7,263},{8... | collective-permute-start | bytes 786440 | tf_op jit(solution)/shard_map/ppermute | solution.py:37
  51.7 39.4 %copy-start.10 = (f32[16,32,128]{2,1,0:T(8,128)}, f32[16,32,128]{2,1,0:T(8,128)S(1)}, u32[]{:S(2)}) copy-start(f32[16,32,128]{2,1,0:T(8,128)S(1)} %copy.153) | copy-start | bytes 786436
  61.6 8.3 %slice-start = ((f32[9,16,32,8]{2,3,1,0:T(8,128)}), f32[3,16,32,8]{2,3,1,0:T(8,128)S(1)}, s32[]{:S(2)}) async-start(f32[9,16,32,8]{2,3,1,0:T(8,128)} %copy-done.19), calls=%async_computation | async-start | bytes 393216 | tf_op jit(solution)/shard_map/slice | solution.py:202
  71.8 3.1 %copy-start.39 = (s32[16,32]{1,0:T(8,128)S(1)}, s32[16,32]{1,0:T(8,128)}, u32[]{:S(2)}) copy-start(s32[16,32]{1,0:T(8,128)} %squeeze.120) | copy-start | bytes 6148
  71.8 3.1 %copy-start.40 = (s32[1024]{0:T(1024)S(1)}, s32[1024]{0:T(1024)}, u32[]{:S(2)}) copy-start(s32[1024]{0:T(1024)} %pad_clamp_fusion.2) | copy-start | bytes 12292
  76.6 9.8 %copy-start.3 = (f32[18,34,130]{2,1,0:T(8,128)S(1)}, f32[18,34,130]{2,1,0:T(8,128)}, u32[]{:S(2)}) copy-start(f32[18,34,130]{2,1,0:T(8,128)} %copy-done.2) | copy-start | bytes 954724
  76.6 9.9 %copy-start.5 = (f32[18,34,130]{2,1,0:T(8,128)S(1)}, f32[18,34,130]{2,1,0:T(8,128)}, u32[]{:S(2)}) copy-start(f32[18,34,130]{2,1,0:T(8,128)} %copy-done.4) | copy-start | bytes 954724
  79.5 8.2 %collective-permute-start.3 = (f32[18,1,128]{2,1,0:T(1,128)S(1)}, f32[18,1,128]{2,1,0:T(1,128)S(1)}, u32[]{:S(2)}, u32[]{:S(2)}) collective-permute-start(f32[18,1,128]{2,1,0:T(1,128)S(1)} %get-tuple-element.112), channel_id=1, source_target_pairs={{0,1},{1,0},{2,3},{3,2},{4,5},{5,4},{6,7},{7,6},{8,9},{9,8},{10,11... | collective-permute-start | bytes 27656 | tf_op jit(solution)/shard_map/ppermute | solution.py:26
  83.1 8.0 %copy-start.12 = (f32[16,32,128]{2,1,0:T(8,128)S(1)}, f32[16,32,128]{2,1,0:T(8,128)}, u32[]{:S(2)}) copy-start(f32[16,32,128]{2,1,0:T(8,128)} %copy.158) | copy-start | bytes 786436
  83.1 8.0 %copy-start.13 = (f32[16,32,128]{2,1,0:T(8,128)S(1)}, f32[16,32,128]{2,1,0:T(8,128)}, u32[]{:S(2)}) copy-start(f32[16,32,128]{2,1,0:T(8,128)} %copy.157) | copy-start | bytes 786436
  83.1 8.0 %copy-start.14 = (f32[16,32,128]{2,1,0:T(8,128)S(1)}, f32[16,32,128]{2,1,0:T(8,128)}, u32[]{:S(2)}) copy-start(f32[16,32,128]{2,1,0:T(8,128)} %copy.156) | copy-start | bytes 786436
  83.1 8.0 %copy-start.15 = (f32[16,32,128]{2,1,0:T(8,128)S(1)}, f32[16,32,128]{2,1,0:T(8,128)}, u32[]{:S(2)}) copy-start(f32[16,32,128]{2,1,0:T(8,128)} %copy.155) | copy-start | bytes 786436
  83.2 8.0 %copy-start.16 = (f32[16,32,128]{2,1,0:T(8,128)S(1)}, f32[16,32,128]{2,1,0:T(8,128)}, u32[]{:S(2)}) copy-start(f32[16,32,128]{2,1,0:T(8,128)} %copy.154) | copy-start | bytes 786436
  83.2 8.0 %copy-start.23 = (f32[16,32,128]{2,1,0:T(8,128)S(1)}, f32[16,32,128]{2,1,0:T(8,128)}, u32[]{:S(2)}) copy-start(f32[16,32,128]{2,1,0:T(8,128)} %get-tuple-element.75) | copy-start | bytes 786436
  83.2 6.0 %collective-permute-start.2 = (f32[18,1,128]{2,1,0:T(1,128)S(1)}, f32[18,1,128]{2,1,0:T(1,128)S(1)}, u32[]{:S(2)}, u32[]{:S(2)}) collective-permute-start(f32[18,1,128]{2,1,0:T(1,128)S(1)} %get-tuple-element.113), channel_id=1, source_target_pairs={{1,0},{0,1},{3,2},{2,3},{5,4},{4,5},{7,6},{6,7},{9,8},{8,9},{11,10... | collective-permute-start | bytes 27656 | tf_op jit(solution)/shard_map/ppermute | solution.py:29
  91.2 2.5 %copy-start.20 = (f32[512,128]{1,0:T(8,128)S(1)}, f32[512,128]{1,0:T(8,128)}, u32[]{:S(2)}) copy-start(f32[512,128]{1,0:T(8,128)} %gather_fusion) | copy-start | bytes 786436
  95.2 30.4 %copy-start.17 = (f32[16,32,128]{2,1,0:T(8,128)}, f32[16,32,128]{2,1,0:T(8,128)S(1)}, u32[]{:S(2)}) copy-start(f32[16,32,128]{2,1,0:T(8,128)S(1)} %get-tuple-element.82) | copy-start | bytes 786436
  95.2 12.1 %collective-permute-start.5 = (f32[1,32,128]{2,1,0:T(8,128)S(1)}, f32[1,32,128]{2,1,0:T(8,128)S(1)}, u32[]{:S(2)}, u32[]{:S(2)}) collective-permute-start(f32[1,32,128]{2,1,0:T(8,128)S(1)} %get-tuple-element.114), channel_id=1, source_target_pairs={{0,2},{2,4},{4,6},{6,8},{8,10},{10,12},{12,14},{14,16},{16,18},{18... | collective-permute-start | bytes 49160 | tf_op jit(solution)/shard_map/ppermute | solution.py:26
  97.1 10.9 %collective-permute-start.4 = (f32[1,32,128]{2,1,0:T(8,128)S(1)}, f32[1,32,128]{2,1,0:T(8,128)S(1)}, u32[]{:S(2)}, u32[]{:S(2)}) collective-permute-start(f32[1,32,128]{2,1,0:T(8,128)S(1)} %get-tuple-element.115), channel_id=1, source_target_pairs={{2,0},{4,2},{6,4},{8,6},{10,8},{12,10},{14,12},{16,14},{18,16},{20... | collective-permute-start | bytes 49160 | tf_op jit(solution)/shard_map/ppermute | solution.py:29
  107.2 18.3 %copy-start.11 = (f32[16,32,128]{2,1,0:T(8,128)S(1)}, f32[16,32,128]{2,1,0:T(8,128)}, u32[]{:S(2)}) copy-start(f32[16,32,128]{2,1,0:T(8,128)} %copy-done.10) | copy-start | bytes 786436
  107.3 20.0 %copy-start.24 = (f32[3,16,32,128]{3,2,1,0:T(8,128)}, f32[3,16,32,128]{3,2,1,0:T(8,128)S(1)}, u32[]{:S(2)}) copy-start(f32[3,16,32,128]{3,2,1,0:T(8,128)S(1)} %broadcast_multiply_fusion) | copy-start | bytes 2359300
  108.1 17.1 %collective-permute-start.7 = (f32[18,1,128]{2,1,0:T(1,128)S(1)}, f32[18,1,128]{2,1,0:T(1,128)S(1)}, u32[]{:S(2)}, u32[]{:S(2)}) collective-permute-start(f32[18,1,128]{2,1,0:T(1,128)S(1)} %get-tuple-element.108), channel_id=1, source_target_pairs={{0,1},{1,0},{2,3},{3,2},{4,5},{5,4},{6,7},{7,6},{8,9},{9,8},{10,11... | collective-permute-start | bytes 27656 | tf_op jit(solution)/shard_map/ppermute | solution.py:26
  111.2 13.9 %collective-permute-start.6 = (f32[18,1,128]{2,1,0:T(1,128)S(1)}, f32[18,1,128]{2,1,0:T(1,128)S(1)}, u32[]{:S(2)}, u32[]{:S(2)}) collective-permute-start(f32[18,1,128]{2,1,0:T(1,128)S(1)} %get-tuple-element.109), channel_id=1, source_target_pairs={{1,0},{0,1},{3,2},{2,3},{5,4},{4,5},{7,6},{6,7},{9,8},{8,9},{11,10... | collective-permute-start | bytes 27656 | tf_op jit(solution)/shard_map/ppermute | solution.py:29
  114.9 12.4 %collective-permute-start.10 = (f32[3,1,32,128]{3,2,1,0:T(8,128)S(1)}, f32[3,1,32,128]{3,2,1,0:T(8,128)S(1)}, u32[]{:S(2)}, u32[]{:S(2)}) collective-permute-start(f32[3,1,32,128]{3,2,1,0:T(8,128)S(1)} %get-tuple-element.96), channel_id=1, source_target_pairs={{2,0},{4,2},{6,4},{8,6},{10,8},{12,10},{14,12},{16,14},{18,16},{20... | collective-permute-start | bytes 147464 | tf_op jit(solution)/shard_map/ppermute | solution.py:29
  123.0 7.1 %collective-permute-start.9 = (f32[3,1,32,128]{3,2,0,1:T(8,128)S(1)}, f32[3,1,32,128]{3,2,0,1:T(8,128)S(1)}, u32[]{:S(2)}, u32[]{:S(2)}) collective-permute-start(f32[3,1,32,128]{3,2,0,1:T(8,128)S(1)} %get-tuple-element.97), channel_id=1, source_target_pairs={{0,2},{2,4},{4,6},{6,8},{8,10},{10,12},{12,14},{14,16},{16,18},{18... | collective-permute-start | bytes 147464 | tf_op jit(solution)/shard_map/ppermute | solution.py:26
  125.6 6.1 %copy-start.43 = (pred[32]{0:T(512)(128)(4,1)S(1)}, pred[32]{0:T(512)(128)(4,1)}, u32[]{:S(2)}) copy-start(pred[32]{0:T(512)(128)(4,1)} %get-tuple-element.116) | copy-start | bytes 100
  125.6 7.0 %copy-start.42 = (pred[32]{0:T(512)(128)(4,1)S(1)}, pred[32]{0:T(512)(128)(4,1)}, u32[]{:S(2)}) copy-start(pred[32]{0:T(512)(128)(4,1)} %get-tuple-element.54) | copy-start | bytes 100
  125.6 7.9 %copy-start.7 = (f32[3,16,32,128]{3,2,1,0:T(8,128)S(1)}, f32[3,16,32,128]{3,2,1,0:T(8,128)}, u32[]{:S(2)}) copy-start(f32[3,16,32,128]{3,2,1,0:T(8,128)} %copy-done.6) | copy-start | bytes 2359300
  125.6 7.9 %copy-start.31 = (f32[3,1,32,128]{3,2,1,0:T(8,128)S(1)}, f32[3,1,32,128]{3,2,1,0:T(8,128)}, u32[]{:S(2)}) copy-start(f32[3,1,32,128]{3,2,1,0:T(8,128)} %copy-done.30) | copy-start | bytes 147460
  125.6 7.9 %copy-start.33 = (f32[3,1,32,128]{3,2,1,0:T(8,128)S(1)}, f32[3,1,32,128]{3,2,1,0:T(8,128)}, u32[]{:S(2)}) copy-start(f32[3,1,32,128]{3,2,1,0:T(8,128)} %copy-done.32) | copy-start | bytes 147460
  125.6 7.9 %copy-start.35 = (f32[3,18,1,128]{3,2,1,0:T(1,128)S(1)}, f32[3,18,1,128]{3,2,1,0:T(1,128)}, u32[]{:S(2)}) copy-start(f32[3,18,1,128]{3,2,1,0:T(1,128)} %copy-done.34) | copy-start | bytes 82948
  125.6 7.9 %copy-start.37 = (f32[3,18,1,128]{3,2,1,0:T(1,128)S(1)}, f32[3,18,1,128]{3,2,1,0:T(1,128)}, u32[]{:S(2)}) copy-start(f32[3,18,1,128]{3,2,1,0:T(1,128)} %copy-done.36) | copy-start | bytes 82948
  133.5 3.7 %copy-start.18 = (f32[16,32,128]{2,1,0:T(8,128)S(1)}, f32[16,32,128]{2,1,0:T(8,128)}, u32[]{:S(2)}) copy-start(f32[16,32,128]{2,1,0:T(8,128)} %copy-done.17) | copy-start | bytes 786436
  137.4 18.9 %collective-permute-start.18 = (f32[3,1,32,128]{3,2,1,0:T(8,128)S(1)}, f32[3,1,32,128]{3,2,1,0:T(8,128)S(1)}, u32[]{:S(2)}, u32[]{:S(2)}) collective-permute-start(f32[3,1,32,128]{3,2,1,0:T(8,128)S(1)} %get-tuple-element.94), channel_id=1, source_target_pairs={{0,2},{2,4},{4,6},{6,8},{8,10},{10,12},{12,14},{14,16},{16,18},{18... | collective-permute-start | bytes 147464 | tf_op jit(solution)/shard_map/ppermute | solution.py:26
  139.3 16.9 %collective-permute-start.17 = (f32[3,1,32,128]{3,2,1,0:T(8,128)S(1)}, f32[3,1,32,128]{3,2,1,0:T(8,128)S(1)}, u32[]{:S(2)}, u32[]{:S(2)}) collective-permute-start(f32[3,1,32,128]{3,2,1,0:T(8,128)S(1)} %get-tuple-element.95), channel_id=1, source_target_pairs={{2,0},{4,2},{6,4},{8,6},{10,8},{12,10},{14,12},{16,14},{18,16},{20... | collective-permute-start | bytes 147464 | tf_op jit(solution)/shard_map/ppermute | solution.py:29
  147.3 15.8 %collective-permute-start.16 = (f32[3,1,32,128]{3,2,0,1:T(8,128)S(1)}, f32[3,1,32,128]{3,2,0,1:T(8,128)S(1)}, u32[]{:S(2)}, u32[]{:S(2)}) collective-permute-start(f32[3,1,32,128]{3,2,0,1:T(8,128)S(1)} %get-tuple-element.92), channel_id=1, source_target_pairs={{2,0},{4,2},{6,4},{8,6},{10,8},{12,10},{14,12},{16,14},{18,16},{20... | collective-permute-start | bytes 147464 | tf_op jit(solution)/shard_map/ppermute | solution.py:29
  154.3 9.6 %collective-permute-start.15 = (f32[3,1,32,128]{3,2,0,1:T(8,128)S(1)}, f32[3,1,32,128]{3,2,0,1:T(8,128)S(1)}, u32[]{:S(2)}, u32[]{:S(2)}) collective-permute-start(f32[3,1,32,128]{3,2,0,1:T(8,128)S(1)} %get-tuple-element.93), channel_id=1, source_target_pairs={{0,2},{2,4},{4,6},{6,8},{8,10},{10,12},{12,14},{14,16},{16,18},{18... | collective-permute-start | bytes 147464 | tf_op jit(solution)/shard_map/ppermute | solution.py:26
  156.3 8.6 %collective-permute-start.20 = (f32[3,18,1,128]{3,2,1,0:T(1,128)S(1)}, f32[3,18,1,128]{3,2,1,0:T(1,128)S(1)}, u32[]{:S(2)}, u32[]{:S(2)}) collective-permute-start(f32[3,18,1,128]{3,2,1,0:T(1,128)S(1)} %get-tuple-element.88), channel_id=1, source_target_pairs={{0,1},{1,0},{2,3},{3,2},{4,5},{5,4},{6,7},{7,6},{8,9},{9,8},{10,11... | collective-permute-start | bytes 82952 | tf_op jit(solution)/shard_map/ppermute | solution.py:26
  159.5 6.1 %collective-permute-start.19 = (f32[3,18,1,128]{3,2,1,0:T(1,128)S(1)}, f32[3,18,1,128]{3,2,1,0:T(1,128)S(1)}, u32[]{:S(2)}, u32[]{:S(2)}) collective-permute-start(f32[3,18,1,128]{3,2,1,0:T(1,128)S(1)} %get-tuple-element.89), channel_id=1, source_target_pairs={{1,0},{0,1},{3,2},{2,3},{5,4},{4,5},{7,6},{6,7},{9,8},{8,9},{11,10... | collective-permute-start | bytes 82952 | tf_op jit(solution)/shard_map/ppermute | solution.py:29
  167.8 1.1 copy-start.8
  167.8 1.4 copy-start.9
  167.8 1.4 copy-start.21
  167.9 1.5 copy-start.22
  169.3 1.2 copy-start.28
  169.3 1.3 copy-start.29
  (4 other events, 4.2 us)
where the time goes:
time: 173 us; the launch traced here: 172 us
  starting transfers between devices  91.1 us (53%)
  local copies, waits for them, and re-layouts  40.1 us (23%)
  other arithmetic  30.6 us (18%)
  waiting for transfers between devices  9.04 us (5%)
    ppermute x10, starting transfers between devices, extended_2(): lax.ppermute(lax.slice_in_dim(block, 0, width, axis=dim), axis, backward)  59.1 us
    ppermute x10, starting transfers between devices, extended_2(): lax.ppermute(lax.slice_in_dim(block, block.shape[dim] - width, None, axis...  29.7 us
    broadcast_in_dim x10, local copies, waits for them, and re-layouts, cell_values(): widened = jnp.broadcast_to(picked[..., None], picked.shape + (block_depth,))  15.9 us
    mul x3, local copies, waits for them, and re-layouts, diffuse(): 2.0 * cell_fiber[slot_index]  6.68 us
    ppermute x10, waiting for transfers between devices, extended_2(): lax.ppermute(lax.slice_in_dim(block, 0, width, axis=dim), axis, backward)  6.24 us
    slice x4, local copies, waits for them, and re-layouts, local(): drive = own_data[3:6] + activity * cell_fiber[0:3]  5.59 us
    concatenate x10, other arithmetic, extended_2(): block = jnp.concatenate([low, block, high], axis=dim)  4.92 us
    unnamed x93, local copies, waits for them, and re-layouts  4.48 us
  transfers between devices with their start and end apart: 21, of which 5 were waited for; matrix products, arithmetic and copies ran while one was open for 27% of the time, Pallas kernels for 0%

commit v1 on v0

v1 whole, which is shorter than its diff:
```python
import functools

import jax
import jax.numpy as jnp
from jax import lax
from jax.experimental import pallas as pl
from jax.experimental.pallas import tpu as pltpu
from jax.sharding import PartitionSpec as P

MESH = pl.DeviceIdType.MESH
F32, BF16 = jnp.float32, jnp.bfloat16

CX, CY, NZ = 16, 32, 128
COLS = CX * CY
TOP = COLS + CY
EXT = COLS + 2 * CY
CLASSES = 8
DT = 0.1

CHUNKS = (((1, 5), ((1, 4),)), ((5, 9), ((4, 8),)), ((9, 13), ((8, 12),)), ((13, 15), ((12, 15), (0, 1), (15, 16))))

LEFT, RIGHT, ACROSS, DIAG_LEFT, DIAG_RIGHT, STIFF_LEFT, STIFF_RIGHT = range(7)
TEN_FIRST, TEN_LAST, TEN_ROWS, TEN_BULK = 16, 17, 18, 19
N_COPIES = TEN_BULK + len(CHUNKS)


def rows_of(x, count=1):
    if isinstance(x, int):
        return pl.ds(x * CY, count * CY)
    return pl.ds(pl.multiple_of(x * CY, CY), count * CY)


def lanes():
    return lax.broadcasted_iota(jnp.int32, (CY, NZ), 1)


def sublanes():
    return lax.broadcasted_iota(jnp.int32, (CY, NZ), 0)


def z_up(a):
    return jnp.where(lanes() == NZ - 1, 0.0, pltpu.roll(a, NZ - 1, 1))


def z_down(a):
    return jnp.where(lanes() == 0, 0.0, pltpu.roll(a, 1, 1))


def y_up(a, row):
    return jnp.where(sublanes() == CY - 1, jnp.broadcast_to(row, (CY, NZ)), pltpu.roll(a, CY - 1, 0))


def y_down(a, row):
    return jnp.where(sublanes() == 0, jnp.broadcast_to(row, (CY, NZ)), pltpu.roll(a, 1, 0))


def sig(v):
    return 1.0 / (1.0 + jnp.exp(-v))


def split3(a):
    high = a.astype(BF16)
    rest = a - high.astype(F32)
    mid = rest.astype(BF16)
    low = (rest - mid.astype(F32)).astype(BF16)
    return high, mid, low


def kernel(n_gx, sec_ref, ang_ref, cls_ref, rmap_ref, irow_ref, out_ref,
           inp, ext0, ext1, fib, base, outb, clsx, tbuf, trow, perm, parts, rperm, tie, tbl,
           halo, ypk, corner_out, corner_in, hal, kx, ang, cls, rmap, irow,
           load_sem, send_sem, recv_sem, out_sem):
    sec, gx, gy = lax.axis_index("sec"), lax.axis_index("gx"), lax.axis_index("gy")
    left, right = lax.rem(gx + n_gx - 1, n_gx), lax.rem(gx + 1, n_gx)
    across = 1 - gy
    near = {
        LEFT: (sec, left, gy), RIGHT: (sec, right, gy), ACROSS: (sec, gx, across),
        DIAG_LEFT: (sec, left, across), DIAG_RIGHT: (sec, right, across),
    }
    near[STIFF_LEFT], near[STIFF_RIGHT] = near[LEFT], near[RIGHT]
    partner = (1 - sec, gx, gy)
    ext = (ext0, ext1)

    barrier = pltpu.get_barrier_semaphore()
    for direction in range(5):
        pl.semaphore_signal(barrier, inc=1, device_id=near[direction], device_id_type=MESH)

    def load(src, dst, slot):
        return pltpu.make_async_copy(src, dst, load_sem.at[slot])

    def remote(src, dst, slot, device):
        return pltpu.make_async_remote_copy(
            src_ref=src, dst_ref=dst, send_sem=send_sem.at[slot], recv_sem=recv_sem.at[slot],
            device_id=device, device_id_type=MESH)

    def store(rows, first, count, slot):
        part = pl.ds(first, count)
        return pltpu.make_async_copy(outb.at[part, rows], out_ref.at[part, rows], out_sem.at[slot])

    def halo_copies(phase, fields):
        first, own = pl.ds(0, fields), ext[phase]
        if phase == 0:
            low, high = sec_ref.at[first, pl.ds(0, CY)], sec_ref.at[first, pl.ds(COLS - CY, CY)]
        else:
            low, high = own.at[first, pl.ds(CY, CY)], own.at[first, pl.ds(COLS, CY)]
        both = pl.ds(0, 2 * fields)
        slot = phase * 8
        return (
            remote(low, own.at[first, pl.ds(TOP, CY)], slot + LEFT, near[LEFT]),
            remote(high, own.at[first, pl.ds(0, CY)], slot + RIGHT, near[RIGHT]),
            remote(ypk.at[phase, both], halo.at[phase, both, pl.ds(8, CX)], slot + ACROSS, near[ACROSS]),
            remote(corner_out.at[phase, 0], corner_in.at[phase, 1], slot + DIAG_LEFT, near[DIAG_LEFT]),
            remote(corner_out.at[phase, 1], corner_in.at[phase, 0], slot + DIAG_RIGHT, near[DIAG_RIGHT]),
        )

    def pack_corners(phase, fields):
        for k in range(2 * fields):
            corner_out[phase, 0, k:k + 1] = ypk[phase, k, 0:1]
            corner_out[phase, 1, k:k + 1] = ypk[phase, k, CX - 1:CX]

    def pack_rows(phase, fields):
        for field in range(fields):
            ypk[phase, field] = ext[phase][field, pl.ds(CY + CY - 1, CX, stride=CY)]
            ypk[phase, fields + field] = ext[phase][field, pl.ds(CY, CX, stride=CY)]

    def unpack_corners(phase, fields):
        for k in range(2 * fields):
            halo[phase, k, 7:8] = corner_in[phase, 0, k:k + 1]
            halo[phase, k, 8 + CX:9 + CX] = corner_in[phase, 1, k:k + 1]

    def halo_row(phase, k):
        return halo[phase, k, 8:8 + CX]

    def halo_diff(phase, k):
        return halo[phase, k, 9:9 + CX] - halo[phase, k, 7:7 + CX]

    def row_at(k, x):
        return hal[k, pl.ds(x, 1)]

    def fiber_table():
        azimuth, elevation = ang[:, 0:1], ang[:, 1:2]
        flat = jnp.cos(elevation)
        for k, value in enumerate((jnp.cos(azimuth) * flat, jnp.sin(azimuth) * flat, jnp.sin(elevation))):
            tbl[k] = jnp.broadcast_to(value, (CLASSES, NZ))

    def expand_classes():
        spread = lax.broadcasted_iota(jnp.int32, (8, NZ), 1) // 16 == lax.broadcasted_iota(jnp.int32, (8, NZ), 0)
        spread = jnp.where(spread, 1.0, 0.0).astype(BF16)
        clsx[...] = jnp.dot(cls[...].astype(F32).astype(BF16), spread, preferred_element_type=F32)

    def fiber_of(x):
        kind = clsx[rows_of(x)]
        bit2 = kind >= 3.5
        kind = jnp.where(bit2, kind - 4.0, kind)
        bit1 = kind >= 1.5
        bit0 = jnp.where(bit1, kind - 2.0, kind) >= 0.5
        fields = []
        for k in range(3):
            pick = [jnp.broadcast_to(tbl[k, c:c + 1], (CY, NZ)) for c in range(CLASSES)]
            pick = [jnp.where(bit0, pick[2 * c + 1], pick[2 * c]) for c in range(4)]
            pick = [jnp.where(bit1, pick[2 * c + 1], pick[2 * c]) for c in range(2)]
            fields.append(jnp.where(bit2, pick[1], pick[0]))
        return fields


    @pl.when(sec == 0)
    def _():
        loads = [load(sec_ref.at[0], ext0.at[0, pl.ds(CY, COLS)], 0)]
        loads += [load(sec_ref.at[k], inp.at[k], k) for k in range(1, 8)]
        load_map = load(rmap_ref, rmap, 8)
        load_cls = load(cls_ref, cls, 9)
        load_ang = load(ang_ref, ang, 10)
        load_map.start()
        for k in (0, 1, 2, 3, 6, 7, 4, 5):
            loads[k].start()
        load_cls.start()
        load_ang.start()

        load_map.wait()
        source = jnp.broadcast_to(rmap[0].astype(F32), (8, COLS)).T[:, 0:1]
        spot = lax.broadcasted_iota(jnp.int32, (COLS, COLS), 1).astype(F32)
        perm[...] = jnp.where(jnp.broadcast_to(source, (COLS, COLS)) == spot, 1.0, 0.0).astype(BF16)

        loads[0].wait()
        pack_rows(0, 1)
        pack_corners(0, 1)
        pl.semaphore_wait(barrier, 6)
        first_halo = halo_copies(0, 1)
        for copy in first_halo:
            copy.start()

        for k in (1, 2, 3, 6, 7):
            loads[k].wait()

        def tension_plane(x, carry):
            rows = rows_of(x)
            v = ext0[0, rows_of(x + 1)]
            c, d, f, b, s = inp[1, rows], inp[2, rows], inp[3, rows], inp[6, rows], inp[7, rows]
            square = c * c
            q = square / (square + 0.25)
            flow = 1.2 * d * f * (v - 2.0)
            binding = 2.0 * c * (1.0 - b) - 0.4 * b
            c = c + DT * (-0.3 * flow - 0.5 * c - binding)
            base[0, rows] = c
            base[1, rows] = q
            base[2, rows] = flow
            inp[6, rows] = b + DT * binding
            s = s + DT * (q - s) / 2.0
            square = c * c
            q = square / (square + 0.25)
            outb[1, rows] = q
            s = s + DT * (q - s) / 2.0
            outb[3, rows] = s
            for k, part in enumerate(split3(s)):
                parts[rows, k * NZ:(k + 1) * NZ] = part
            return carry

        lax.fori_loop(0, CX, tension_plane, 0)
        moved = jnp.dot(perm[...], parts[...], preferred_element_type=F32)
        tbuf[...] = moved[:, 0:NZ] + (moved[:, NZ:2 * NZ] + moved[:, 2 * NZ:])
        trow[0] = tbuf[pl.ds(CY - 1, CX, stride=CY)]
        trow[1] = tbuf[pl.ds(0, CX, stride=CY)]
        tension = [
            remote(tbuf.at[rows_of(0)], tbuf.at[rows_of(0)], TEN_FIRST, partner),
            remote(tbuf.at[rows_of(CX - 1)], tbuf.at[rows_of(CX - 1)], TEN_LAST, partner),
            remote(trow, trow, TEN_ROWS, partner),
        ]
        for k, ((low, high), _) in enumerate(CHUNKS):
            rows = rows_of(low, high - low)
            tension.append(remote(tbuf.at[rows], tbuf.at[rows], TEN_BULK + k, partner))
        for copy in tension:
            copy.start()
        everything = pl.ds(0, COLS)
        out_s = store(everything, 3, 1, 0)
        out_s.start()

        load_ang.wait()
        load_cls.wait()
        fiber_table()
        expand_classes()

        def fiber_plane(x, carry):
            for k, value in enumerate(fiber_of(x)):
                fib[k, rows_of(x)] = value
            return carry

        lax.fori_loop(0, CX, fiber_plane, 0)

        def diffusion(phase, x):
            here = ext[phase]
            c, p, m = here[0, rows_of(x + 1)], here[0, rows_of(x + 2)], here[0, rows_of(x)]
            f0, f1, f2 = fib[0, rows_of(x)], fib[1, rows_of(x)], fib[2, rows_of(x)]
            d = p - m
            yu, yd = y_up(c, row_at(0, x)), y_down(c, row_at(1, x))
            e = yu - yd
            twice = 2.0 * c
            v00 = p + m - twice
            v11 = yu + yd - twice
            v22 = z_up(c) + z_down(c) - twice
            x01 = y_up(d, row_at(2, x)) - y_down(d, row_at(3, x))
            x02 = z_up(d) - z_down(d)
            x12 = z_up(e) - z_down(e)
            along = (f0 * (f0 * v00 + 0.5 * (f1 * x01 + f2 * x02))
                     + f1 * (f1 * v11 + 0.5 * (f2 * x12)) + f2 * f2 * v22)
            return c, 0.25 * (v00 + v11 + v22) + 0.75 * along

        def halo_rows(phase):
            unpack_corners(phase, 1)
            hal[0] = halo_row(phase, 1)
            hal[1] = halo_row(phase, 0)
            hal[2] = halo_diff(phase, 1)
            hal[3] = halo_diff(phase, 0)

        loads[4].wait()
        loads[5].wait()
        for copy in first_halo:
            copy.wait_recv()
        halo_rows(0)

        def first_step(x, carry):
            rows = rows_of(x)
            v, spread = diffusion(0, x)
            d, f, n, r = inp[2, rows], inp[3, rows], inp[4, rows], inp[5, rows]
            flow, q = base[2, rows], base[1, rows]
            current = flow + 0.8 * n * (v + 1.0) + 0.6 * q * r * (v + 1.0) + 0.1 * v
            ext1[0, rows_of(x + 1)] = v + DT * (spread - current)
            inp[2, rows] = d + DT * (sig(2.0 * v + 1.0) - d) / 0.5
            inp[3, rows] = f + DT * (sig(-2.0 * v) - f) / 3.0
            inp[4, rows] = n + DT * (sig(2.0 * v) - n)
            inp[5, rows] = r + DT * (sig(v - 0.5) - r) / 5.0
            return carry

        lax.fori_loop(0, CX, first_step, 0)
        pack_rows(1, 1)
        pack_corners(1, 1)
        second_halo = halo_copies(1, 1)
        for copy in second_halo:
            copy.start()

        def second_ions(x, carry):
            rows = rows_of(x)
            v, c, q = ext1[0, rows_of(x + 1)], base[0, rows], outb[1, rows]
            d, f, n, r, b = inp[2, rows], inp[3, rows], inp[4, rows], inp[5, rows], inp[6, rows]
            flow = 1.2 * d * f * (v - 2.0)
            current = flow + 0.8 * n * (v + 1.0) + 0.6 * q * r * (v + 1.0) + 0.1 * v
            binding = 2.0 * c * (1.0 - b) - 0.4 * b
            base[1, rows] = v - DT * current
            outb[1, rows] = c + DT * (-0.3 * flow - 0.5 * c - binding)
            outb[2, rows] = n + DT * (sig(2.0 * v) - n)
            return carry

        lax.fori_loop(0, CX, second_ions, 0)
        out_ions = store(everything, 1, 2, 1)
        out_ions.start()
        for copy in second_halo:
            copy.wait_recv()
        halo_rows(1)

        def second_step(x, carry):
            rows = rows_of(x)
            _, spread = diffusion(1, x)
            outb[0, rows] = base[1, rows] + DT * spread
            return carry

        lax.fori_loop(0, CX, second_step, 0)
        out_v = store(everything, 0, 1, 2)
        out_v.start()
        for copy in (*first_halo, *second_halo, *tension):
            copy.wait_send()
        for copy in (out_s, out_ions, out_v):
            copy.wait()


    @pl.when(sec == 1)
    def _():
        pl.semaphore_signal(barrier, inc=1, device_id=partner, device_id_type=MESH)
        load_u = load(sec_ref.at[pl.ds(0, 3)], ext0.at[:, pl.ds(CY, COLS)], 0)
        load_rest = load(sec_ref.at[pl.ds(3, 5)], inp.at[pl.ds(3, 5)], 1)
        load_row = load(irow_ref, irow, 8)
        load_cls = load(cls_ref, cls, 9)
        load_ang = load(ang_ref, ang, 10)
        load_u.start()
        load_ang.start()
        load_cls.start()
        load_rest.start()
        load_row.start()

        pl.semaphore_wait(barrier, 5)
        first_halo = halo_copies(0, 3)
        stiff = (
            remote(sec_ref.at[6, pl.ds(0, CY)], kx.at[1], STIFF_LEFT, near[STIFF_LEFT]),
            remote(sec_ref.at[6, pl.ds(COLS - CY, CY)], kx.at[0], STIFF_RIGHT, near[STIFF_RIGHT]),
        )
        for copy in (first_halo[0], first_halo[1], *stiff):
            copy.start()
        load_u.wait()
        pack_rows(0, 3)
        pack_corners(0, 3)
        for copy in first_halo[2:]:
            copy.start()

        load_ang.wait()
        load_cls.wait()
        fiber_table()
        expand_classes()
        load_row.wait()
        for side in range(2):
            source = jnp.broadcast_to(irow[side, 0].astype(F32), (CY, CY)).T
            spot = lax.broadcasted_iota(jnp.int32, (CY, CY), 1).astype(F32)
            rperm[side] = jnp.where(source == spot, 1.0, 0.0).astype(BF16)
        load_rest.wait()

        def weight_plane(x, carry):
            rows = rows_of(x)
            relax = 0.06 / inp[6, rows]
            inp[6, rows] = relax
            drive = relax * inp[7, rows]
            for k, value in enumerate(fiber_of(x)):
                fib[k, rows] = drive * value
                inp[3 + k, rows] = relax * inp[3 + k, rows]
            return carry

        kx_own = (0, CX - 1)
        lax.fori_loop(0, CX, weight_plane, 0)

        def halo_rows(phase):
            unpack_corners(phase, 3)
            for side, sign in ((1, 0.5), (0, -0.5)):
                k = 3 * side
                at = 4 * (1 - side)
                hal[at] = halo_row(phase, k) + sign * halo_diff(phase, k + 1)
                hal[at + 1] = 3.0 * halo_row(phase, k + 1) + sign * halo_diff(phase, k)
                hal[at + 2] = halo_row(phase, k + 1)
                hal[at + 3] = halo_row(phase, k + 2)

        def relaxed(phase, x):
            here = ext[phase]
            mid, p, m = rows_of(x + 1), rows_of(x + 2), rows_of(x)
            c0, c1, c2 = here[0, mid], here[1, mid], here[2, mid]
            p0, p1, p2 = here[0, p], here[1, p], here[2, p]
            m0, m1, m2 = here[0, m], here[1, m], here[2, m]
            d0, d1, d2 = 0.5 * (p0 - m0), 0.5 * (p1 - m1), 0.5 * (p2 - m2)
            y2u, y2d = y_up(c2, row_at(3, x)), y_down(c2, row_at(7, x))
            e1 = 0.5 * (y_up(c1, row_at(2, x)) - y_down(c1, row_at(6, x)))
            e2 = 0.5 * (y2u - y2d)
            t1, t2 = 3.0 * c1, 3.0 * c2
            cross = d0 + e1
            s0 = (3.0 * (p0 + m0) + (y_up(c0 + d1, row_at(0, x)) + y_down(c0 - d1, row_at(4, x)))
                  + (z_up(c0 + d2) + z_down(c0 - d2)))
            s1 = ((p1 + m1) + (y_up(t1 + d0, row_at(1, x)) + y_down(t1 - d0, row_at(5, x)))
                  + (z_up(c1 + e2) + z_down(c1 - e2)))
            s2 = (p2 + m2) + (y2u + y2d) + (z_up(t2 + cross) + z_down(t2 - cross))
            return 0.4 * c0 + 0.06 * s0, 0.4 * c1 + 0.06 * s1, 0.4 * c2 + 0.06 * s2

        def tie_forces(phase):
            here = ext[phase]
            for side in range(2):
                far = pl.ds((0, TOP)[side], CY)
                pieces = []
                for k in range(3):
                    pieces += list(split3((2.0 * kx[side]) * here[k, far]))
                got = jnp.dot(rperm[side], jnp.concatenate(pieces, axis=1), preferred_element_type=F32)
                x = kx_own[side]
                relax = inp[6, rows_of(x)]
                for k in range(3):
                    at = 3 * NZ * k
                    picked = got[:, at:at + NZ] + (got[:, at + NZ:at + 2 * NZ] + got[:, at + 2 * NZ:at + 3 * NZ])
                    tie[side, k] = relax * picked - 0.12 * here[k, rows_of(x + 1)]

        for copy in (*first_halo, *stiff):
            copy.wait_recv()
        halo_rows(0)

        def base_plane(x, carry):
            rows = rows_of(x)
            for k, value in enumerate(relaxed(0, x)):
                base[k, rows] = value + inp[3 + k, rows]
            return carry

        lax.fori_loop(0, CX, base_plane, 0)
        tie_forces(0)
        for side in range(2):
            rows = rows_of(kx_own[side])
            for k in range(3):
                base[k, rows] = base[k, rows] + tie[side, k]

        def receive(slot, ref):
            remote(ref, ref, slot, partner).wait_recv()

        def activate(x):
            rows = rows_of(x)
            tension = tbuf[rows]
            outb[3, rows] = inp[7, rows] * tension
            for k in range(3):
                ext1[k, rows_of(x + 1)] = base[k, rows] + fib[k, rows] * tension

        second_halo = halo_copies(1, 3)
        stores = []
        for side, slot in ((0, TEN_FIRST), (1, TEN_LAST)):
            x = kx_own[side]
            receive(slot, tbuf.at[rows_of(x)])
            activate(x)
            second_halo[side].start()
            stores.append(store(rows_of(x), 3, 1, side))
            stores[-1].start()
        receive(TEN_ROWS, trow)
        for side, y in ((0, CY - 1), (1, 0)):
            for k in range(3):
                own = pl.ds(y, CX, stride=CY)
                ypk[1, 3 * side + k] = base[k, own] + fib[k, own] * trow[side]
        pack_corners(1, 3)
        for copy in second_halo[2:]:
            copy.start()

        def activate_plane(x, carry):
            activate(x)
            return carry

        def last_plane(x, carry):
            rows = rows_of(x)
            tension = tbuf[rows]
            for k, value in enumerate(relaxed(1, x)):
                outb[k, rows] = value + inp[3 + k, rows] + fib[k, rows] * tension
            return carry

        slot = 2
        for index, ((low, high), ready) in enumerate(CHUNKS):
            rows = rows_of(low, high - low)
            receive(TEN_BULK + index, tbuf.at[rows])
            lax.fori_loop(low, high, activate_plane, 0)
            stores.append(store(rows, 3, 1, slot))
            stores[-1].start()
            slot += 1
            if index == 0:
                for copy in second_halo:
                    copy.wait_recv()
                halo_rows(1)
                tie_forces(1)
            for low, high in ready:
                rows = rows_of(low, high - low)
                lax.fori_loop(low, high, last_plane, 0)
                if low in kx_own:
                    side = kx_own.index(low)
                    for k in range(3):
                        outb[k, rows] = outb[k, rows] + tie[side, k]
                stores.append(store(rows, 0, 3, slot))
                stores[-1].start()
                slot += 1
        for copy in (*first_halo, *second_halo, *stiff):
            copy.wait_send()
        for copy in stores:
            copy.wait()


def solution(mesh):
    n_gx = mesh.shape["gx"]

    def local(sections, fiber_angles, fiber_class, row_map, interface_rows):
        vmem = pltpu.VMEM
        field, padded = (COLS, NZ), (EXT, NZ)
        out = pl.pallas_call(
            functools.partial(kernel, n_gx),
            out_shape=jax.ShapeDtypeStruct((4, COLS, NZ), F32),
            in_specs=[pl.BlockSpec(memory_space=pl.ANY)] * 5,
            out_specs=pl.BlockSpec(memory_space=pl.ANY),
            scratch_shapes=[
                vmem((8, *field), F32),
                vmem((3, *padded), F32),
                vmem((3, *padded), F32),
                vmem((3, *field), F32),
                vmem((3, *field), F32),
                vmem((4, *field), F32),
                vmem(field, F32),
                vmem(field, F32),
                vmem((2, CX, NZ), F32),
                vmem((COLS, COLS), BF16),
                vmem((COLS, 3 * NZ), BF16),
                vmem((2, CY, CY), BF16),
                vmem((2, 3, CY, NZ), F32),
                vmem((3, CLASSES, NZ), F32),
                vmem((2, 6, 32, NZ), F32),
                vmem((2, 6, CX, NZ), F32),
                vmem((2, 2, 8, NZ), F32),
                vmem((2, 2, 8, NZ), F32),
                vmem((8, CX, NZ), F32),
                vmem((2, CY, NZ), F32),
                vmem((CLASSES, 2), F32),
                vmem((COLS, 8), jnp.int32),
                vmem((1, 1, COLS), jnp.int32),
                vmem((2, 1, 1, CY), jnp.int32),
                pltpu.SemaphoreType.DMA((11,)),
                pltpu.SemaphoreType.DMA((N_COPIES,)),
                pltpu.SemaphoreType.DMA((N_COPIES,)),
                pltpu.SemaphoreType.DMA((16,)),
            ],
            compiler_params=pltpu.CompilerParams(
                collective_id=0, has_side_effects=True, vmem_limit_bytes=24 * 1024 * 1024),
        )(
            sections.reshape(8, COLS, NZ), fiber_angles, fiber_class.reshape(COLS, 8), row_map, interface_rows
        )
        return out.reshape(1, 4, CX, CY, NZ)

    in_specs = (
        P("sec", None, "gx", "gy", None),
        P(),
        P("gx", "gy", None),
        P("gx", "gy", None),
        P(None, "gx", "gy", None),
    )
    out_specs = P("sec", None, "gx", "gy", None)
    return jax.shard_map(local, mesh=mesh, in_specs=in_specs, out_specs=out_specs, check_vma=False)
```

time: 173 us -> 35.9 us (0.21)
  the two profiles are of different devices: /device:TPU:1 before, /device:TPU:2 now
where the time goes in v1:
time: 35.9 us; the launch traced here: 35.7 us
  Pallas kernels  30 us (84%)
  local copies, waits for them, and re-layouts  5.63 us (16%)
    pallas_call x1, Pallas kernels, local(): pl.pallas_call(functools.partial(kernel, n_gx), out_shape=jax.ShapeDtypeS...  30 us
    unnamed x9, local copies, waits for them, and re-layouts  5.63 us

profile of v1, /device:TPU:2, one launch (start us, length us, event | category | flops | bytes accessed | tf_op | source)
XLA Modules:
  0.0 35.7 jit_solution(10103895734350481639)
XLA Ops:
  0.0 0.8 %copy.7.ang_ref = f32[8,2]{1,0:T(8,128)S(1)} copy(f32[8,2]{0,1:T(2,128)} %param.6) | data formatting | bytes 128 | tf_op args[1]
  0.8 1.0 %copy.6 = s32[16,32,8]{2,1,0:T(8,128)S(1)} copy(s32[16,32,8]{1,2,0:T(8,128)} %param.7) | data formatting | bytes 32768 | tf_op args[2]
  1.7 0.0 copy-start
  1.7 1.6 %copy-done = f32[1,8,16,32,128]{4,3,2,1,0:T(8,128)S(1)} copy-done((f32[1,8,16,32,128]{4,3,2,1,0:T(8,128)S(1)}, f32[1,8,16,32,128]{4,3,2,1,0:T(8,128)}, u32[]{:S(2)}) %copy-start) | copy-done | bytes 2097176
  3.3 0.0 copy-start.1
  3.3 0.7 %copy-done.1 = s32[1,1,512]{2,1,0:T(1,128)S(1)} copy-done((s32[1,1,512]{2,1,0:T(1,128)S(1)}, s32[1,1,512]{2,1,0:T(1,128)}, u32[]{:S(2)}) %copy-start.1) | copy-done | bytes 2072
  4.0 0.0 copy-start.2
  4.0 0.7 %copy-done.2 = s32[2,1,1,32]{3,2,1,0:T(1,128)S(1)} copy-done((s32[2,1,1,32]{3,2,1,0:T(1,128)S(1)}, s32[2,1,1,32]{3,2,1,0:T(1,128)}, u32[]{:S(2)}) %copy-start.2) | copy-done | bytes 280
  4.7 30.0 %shard_map.55 = f32[4,512,128]{2,1,0:T(8,128)S(1)} custom-call(f32[8,512,128]{2,1,0:T(8,128)S(1)} %bitcast.4, f32[8,2]{1,0:T(8,128)S(1)} %copy.7.ang_ref, s32[512,8]{1,0:T(8,128)S(1)} %bitcast.5, s32[1,1,512]{2,1,0:T(1,128)S(1)} %copy-done.1, s32[2,1,1,32]{3,2,1,0:T(1,128)S(1)} %copy-done.2), custom_call_target="tpu_custom_call" | custom-call | tf_op jit(solution)/shard_map/pallas_call | solution.py:521
  34.7 1.0 %copy.9 = f32[1,4,16,32,128]{4,3,2,1,0:T(8,128)} copy(f32[1,4,16,32,128]{4,3,2,1,0:T(8,128)S(1)} %bitcast.3) | data formatting | bytes 2097152
Async XLA Ops:
  1.7 1.6 %copy-start = (f32[1,8,16,32,128]{4,3,2,1,0:T(8,128)S(1)}, f32[1,8,16,32,128]{4,3,2,1,0:T(8,128)}, u32[]{:S(2)}) copy-start(f32[1,8,16,32,128]{4,3,2,1,0:T(8,128)} %param.5) | copy-start | bytes 6291460
  3.3 0.7 %copy-start.1 = (s32[1,1,512]{2,1,0:T(1,128)S(1)}, s32[1,1,512]{2,1,0:T(1,128)}, u32[]{:S(2)}) copy-start(s32[1,1,512]{2,1,0:T(1,128)} %rmap_ref.1) | copy-start | bytes 6148
  4.0 0.7 %copy-start.2 = (s32[2,1,1,32]{3,2,1,0:T(1,128)S(1)}, s32[2,1,1,32]{3,2,1,0:T(1,128)}, u32[]{:S(2)}) copy-start(s32[2,1,1,32]{3,2,1,0:T(1,128)} %irow_ref.1) | copy-start | bytes 772

commit v2 on v1

v2 whole, which is shorter than its diff:
```python
import functools

import jax
import jax.numpy as jnp
from jax import lax
from jax.experimental import pallas as pl
from jax.experimental.pallas import tpu as pltpu
from jax.sharding import PartitionSpec as P

MESH = pl.DeviceIdType.MESH
F32, BF16 = jnp.float32, jnp.bfloat16

CX, CY, NZ = 16, 32, 128
COLS = CX * CY
TOP = COLS + CY
EXT = COLS + 2 * CY
CLASSES = 8
DT = 0.1

CHUNKS = (((1, 5), (1, 4)), ((5, 9), (4, 8)), ((9, 13), (8, 12)), ((13, 15), (12, 14)))

LEFT, RIGHT, ACROSS, DIAG_LEFT, DIAG_RIGHT, STIFF_LEFT, STIFF_RIGHT = range(7)
TEN_FIRST, TEN_LAST, TEN_ROWS, TEN_BULK = 16, 17, 18, 19
N_COPIES = TEN_BULK + len(CHUNKS)
ENDS = (0, CX - 1)


def rows_of(x, count=1):
    if isinstance(x, int):
        return pl.ds(x * CY, count * CY)
    return pl.ds(pl.multiple_of(x * CY, CY), count * CY)


def lanes():
    return lax.broadcasted_iota(jnp.int32, (CY, NZ), 1)


def sublanes():
    return lax.broadcasted_iota(jnp.int32, (CY, NZ), 0)


def z_up(a):
    return jnp.where(lanes() == NZ - 1, 0.0, pltpu.roll(a, NZ - 1, 1))


def z_down(a):
    return jnp.where(lanes() == 0, 0.0, pltpu.roll(a, 1, 1))


def y_up(a, row):
    return jnp.where(sublanes() == CY - 1, jnp.broadcast_to(row, (CY, NZ)), pltpu.roll(a, CY - 1, 0))


def y_down(a, row):
    return jnp.where(sublanes() == 0, jnp.broadcast_to(row, (CY, NZ)), pltpu.roll(a, 1, 0))


def sig(v):
    return 1.0 / (1.0 + jnp.exp(-v))


def split3(a):
    high = a.astype(BF16)
    rest = a - high.astype(F32)
    mid = rest.astype(BF16)
    low = (rest - mid.astype(F32)).astype(BF16)
    return high, mid, low


def kernel(n_gx, sec_ref, ang_ref, cls_ref, rmap_ref, irow_ref, out_ref,
           inp, ext0, ext1, fib, base, packed, tbuf, trow, perm, parts, rperm, tie,
           halo, ypk, corner_out, corner_in, hal, kx, ang, cls, rmap, irow,
           load_sem, send_sem, recv_sem):
    sec, gx, gy = lax.axis_index("sec"), lax.axis_index("gx"), lax.axis_index("gy")
    left, right = lax.rem(gx + n_gx - 1, n_gx), lax.rem(gx + 1, n_gx)
    across = 1 - gy
    near = {
        LEFT: (sec, left, gy), RIGHT: (sec, right, gy), ACROSS: (sec, gx, across),
        DIAG_LEFT: (sec, left, across), DIAG_RIGHT: (sec, right, across),
    }
    near[STIFF_LEFT], near[STIFF_RIGHT] = near[LEFT], near[RIGHT]
    partner = (1 - sec, gx, gy)
    ext = (ext0, ext1)

    barrier = pltpu.get_barrier_semaphore()
    for direction in range(5):
        pl.semaphore_signal(barrier, inc=1, device_id=near[direction], device_id_type=MESH)

    def load(src, dst, slot):
        return pltpu.make_async_copy(src, dst, load_sem.at[slot])

    def remote(src, dst, slot, device):
        return pltpu.make_async_remote_copy(
            src_ref=src, dst_ref=dst, send_sem=send_sem.at[slot], recv_sem=recv_sem.at[slot],
            device_id=device, device_id_type=MESH)

    def halo_copies(phase, fields):
        first, own = pl.ds(0, fields), ext[phase]
        if phase == 0:
            low, high = sec_ref.at[first, pl.ds(0, CY)], sec_ref.at[first, pl.ds(COLS - CY, CY)]
        else:
            low, high = own.at[first, pl.ds(CY, CY)], own.at[first, pl.ds(COLS, CY)]
        both = pl.ds(0, 2 * fields)
        slot = phase * 8
        return (
            remote(low, own.at[first, pl.ds(TOP, CY)], slot + LEFT, near[LEFT]),
            remote(high, own.at[first, pl.ds(0, CY)], slot + RIGHT, near[RIGHT]),
            remote(ypk.at[phase, both], halo.at[phase, both, pl.ds(8, CX)], slot + ACROSS, near[ACROSS]),
            remote(corner_out.at[phase, 0], corner_in.at[phase, 1], slot + DIAG_LEFT, near[DIAG_LEFT]),
            remote(corner_out.at[phase, 1], corner_in.at[phase, 0], slot + DIAG_RIGHT, near[DIAG_RIGHT]),
        )

    def pack_corners(phase, fields, side):
        for k in range(fields):
            for part, y in ((0, CY - 1), (1, 0)):
                row = CY + ENDS[side] * CY + y
                at = part * fields + k
                corner_out[phase, side, at:at + 1] = ext[phase][k, row:row + 1]

    def pack_rows(phase, fields):
        for field in range(fields):
            ypk[phase, field] = ext[phase][field, pl.ds(CY + CY - 1, CX, stride=CY)]
            ypk[phase, fields + field] = ext[phase][field, pl.ds(CY, CX, stride=CY)]

    def wait_side(copies, side):
        copies[1 - side].wait_recv()
        copies[DIAG_RIGHT - side].wait_recv()

    def unpack_corners(phase, fields, side):
        row = (7, 8 + CX)[side]
        for k in range(2 * fields):
            halo[phase, k, row:row + 1] = corner_in[phase, side, k:k + 1]

    def halo_row(phase, k):
        return halo[phase, k, 8:8 + CX]

    def halo_diff(phase, k):
        return halo[phase, k, 9:9 + CX] - halo[phase, k, 7:7 + CX]

    def row_at(k, x):
        return hal[k, pl.ds(x, 1)]

    def pack_fibers():
        azimuth, elevation = ang[0:1, :], ang[1:2, :]
        flat = jnp.cos(elevation)
        table = (jnp.cos(azimuth) * flat, jnp.sin(azimuth) * flat, jnp.sin(elevation))
        kind = cls[...].astype(F32).T
        for k, value in enumerate(table):
            total = jnp.broadcast_to(value[:, 0:1], (CY, NZ))
            for c in range(1, CLASSES):
                total = jnp.where(kind == float(c), jnp.broadcast_to(value[:, c:c + 1], (CY, NZ)), total)
            packed[k] = total

    def fiber_of(x):
        place = lanes() // 16 + 8 * x
        return [jnp.take_along_axis(packed[k], place, axis=1) for k in range(3)]


    @pl.when(sec == 0)
    def _():
        loads = [load(sec_ref.at[0], ext0.at[0, pl.ds(CY, COLS)], 0)]
        loads += [load(sec_ref.at[k], inp.at[k], k) for k in range(1, 8)]
        load_map = load(rmap_ref, rmap, 8)
        load_cls = load(cls_ref, cls, 9)
        load_ang = load(ang_ref, ang, 10)
        load_map.start()
        for k in (0, 1, 2, 3, 6, 7):
            loads[k].start()
        load_cls.start()
        load_ang.start()
        loads[4].start()
        loads[5].start()

        load_map.wait()
        source = jnp.broadcast_to(rmap[0].astype(F32), (8, COLS)).T[:, 0:1]
        spot = lax.broadcasted_iota(jnp.int32, (COLS, COLS), 1).astype(F32)
        perm[...] = jnp.where(jnp.broadcast_to(source, (COLS, COLS)) == spot, 1.0, 0.0).astype(BF16)

        for k in (0, 1, 2, 3, 6, 7):
            loads[k].wait()

        def tension_plane(x, carry):
            rows = rows_of(x)
            v = ext0[0, rows_of(x + 1)]
            c, d, f, b, s = inp[1, rows], inp[2, rows], inp[3, rows], inp[6, rows], inp[7, rows]
            square = c * c
            q = square / (square + 0.25)
            flow = 1.2 * d * f * (v - 2.0)
            binding = 2.0 * c * (1.0 - b) - 0.4 * b
            c = c + DT * (-0.3 * flow - 0.5 * c - binding)
            base[0, rows] = c
            base[1, rows] = q
            base[2, rows] = flow
            inp[6, rows] = b + DT * binding
            s = s + DT * (q - s) / 2.0
            square = c * c
            q = square / (square + 0.25)
            out_ref[1, rows] = q
            s = s + DT * (q - s) / 2.0
            out_ref[3, rows] = s
            for k, part in enumerate(split3(s)):
                parts[rows, k * NZ:(k + 1) * NZ] = part
            return carry

        lax.fori_loop(0, CX, tension_plane, 0)

        def permuted(low, high):
            moved = jnp.dot(perm[low * CY:high * CY], parts[...], preferred_element_type=F32)
            tbuf[low * CY:high * CY] = moved[:, 0:NZ] + (moved[:, NZ:2 * NZ] + moved[:, 2 * NZ:])

        permuted(CX - 1, CX)
        permuted(0, CX - 1)
        trow[0] = tbuf[pl.ds(CY - 1, CX, stride=CY)]
        trow[1] = tbuf[pl.ds(0, CX, stride=CY)]
        pack_rows(0, 1)
        pack_corners(0, 1, 0)
        pack_corners(0, 1, 1)

        pl.semaphore_wait(barrier, 6)
        first_halo = halo_copies(0, 1)
        for copy in first_halo:
            copy.start()
        tension = [
            remote(tbuf.at[rows_of(CX - 1)], tbuf.at[rows_of(CX - 1)], TEN_LAST, partner),
            remote(tbuf.at[rows_of(0)], tbuf.at[rows_of(0)], TEN_FIRST, partner),
            remote(trow, trow, TEN_ROWS, partner),
        ]
        for k, ((low, high), _) in enumerate(CHUNKS):
            rows = rows_of(low, high - low)
            tension.append(remote(tbuf.at[rows], tbuf.at[rows], TEN_BULK + k, partner))
        for copy in tension:
            copy.start()

        load_ang.wait()
        load_cls.wait()
        pack_fibers()

        def fiber_plane(x, carry):
            for k, value in enumerate(fiber_of(x)):
                fib[k, rows_of(x)] = value
            return carry

        lax.fori_loop(0, CX, fiber_plane, 0)

        def diffusion(phase, x):
            here = ext[phase]
            c, p, m = here[0, rows_of(x + 1)], here[0, rows_of(x + 2)], here[0, rows_of(x)]
            f0, f1, f2 = fib[0, rows_of(x)], fib[1, rows_of(x)], fib[2, rows_of(x)]
            d = p - m
            yu, yd = y_up(c, row_at(0, x)), y_down(c, row_at(1, x))
            e = yu - yd
            twice = 2.0 * c
            v00 = p + m - twice
            v11 = yu + yd - twice
            v22 = z_up(c) + z_down(c) - twice
            x01 = y_up(d, row_at(2, x)) - y_down(d, row_at(3, x))
            x02 = z_up(d) - z_down(d)
            x12 = z_up(e) - z_down(e)
            along = (f0 * (f0 * v00 + 0.5 * (f1 * x01 + f2 * x02))
                     + f1 * (f1 * v11 + 0.5 * (f2 * x12)) + f2 * f2 * v22)
            return c, 0.25 * (v00 + v11 + v22) + 0.75 * along

        def halo_rows(phase):
            hal[0] = halo_row(phase, 1)
            hal[1] = halo_row(phase, 0)
            hal[2] = halo_diff(phase, 1)
            hal[3] = halo_diff(phase, 0)

        loads[4].wait()
        loads[5].wait()

        def first_step(x, carry):
            rows = rows_of(x)
            v, spread = diffusion(0, x)
            d, f, n, r = inp[2, rows], inp[3, rows], inp[4, rows], inp[5, rows]
            flow, q = base[2, rows], base[1, rows]
            current = flow + 0.8 * n * (v + 1.0) + 0.6 * q * r * (v + 1.0) + 0.1 * v
            ext1[0, rows_of(x + 1)] = v + DT * (spread - current)
            inp[2, rows] = d + DT * (sig(2.0 * v + 1.0) - d) / 0.5
            inp[3, rows] = f + DT * (sig(-2.0 * v) - f) / 3.0
            inp[4, rows] = n + DT * (sig(2.0 * v) - n)
            inp[5, rows] = r + DT * (sig(v - 0.5) - r) / 5.0
            return carry

        first_halo[ACROSS].wait_recv()
        halo_rows(0)
        lax.fori_loop(1, CX - 1, first_step, 0)
        second_halo = halo_copies(1, 1)
        for side in (1, 0):
            wait_side(first_halo, side)
            unpack_corners(0, 1, side)
            halo_rows(0)
            first_step(ENDS[side], 0)
            pack_corners(1, 1, side)
            second_halo[side].start()
            second_halo[DIAG_LEFT + side].start()
        pack_rows(1, 1)
        second_halo[ACROSS].start()

        def second_ions(x, carry):
            rows = rows_of(x)
            v, c, q = ext1[0, rows_of(x + 1)], base[0, rows], out_ref[1, rows]
            d, f, n, r, b = inp[2, rows], inp[3, rows], inp[4, rows], inp[5, rows], inp[6, rows]
            flow = 1.2 * d * f * (v - 2.0)
            current = flow + 0.8 * n * (v + 1.0) + 0.6 * q * r * (v + 1.0) + 0.1 * v
            binding = 2.0 * c * (1.0 - b) - 0.4 * b
            base[1, rows] = v - DT * current
            out_ref[1, rows] = c + DT * (-0.3 * flow - 0.5 * c - binding)
            out_ref[2, rows] = n + DT * (sig(2.0 * v) - n)
            return carry

        lax.fori_loop(0, CX, second_ions, 0)

        def second_step(x, carry):
            rows = rows_of(x)
            _, spread = diffusion(1, x)
            out_ref[0, rows] = base[1, rows] + DT * spread
            return carry

        second_halo[ACROSS].wait_recv()
        halo_rows(1)
        lax.fori_loop(1, CX - 1, second_step, 0)
        for side in (1, 0):
            wait_side(second_halo, side)
            unpack_corners(1, 1, side)
            halo_rows(1)
            second_step(ENDS[side], 0)
        for copy in (*first_halo, *second_halo, *tension):
            copy.wait_send()


    @pl.when(sec == 1)
    def _():
        pl.semaphore_signal(barrier, inc=1, device_id=partner, device_id_type=MESH)
        load_u = load(sec_ref.at[pl.ds(0, 3)], ext0.at[:, pl.ds(CY, COLS)], 0)
        load_rest = load(sec_ref.at[pl.ds(3, 5)], inp.at[pl.ds(3, 5)], 1)
        load_row = load(irow_ref, irow, 8)
        load_cls = load(cls_ref, cls, 9)
        load_ang = load(ang_ref, ang, 10)
        load_ang.start()
        load_cls.start()
        load_row.start()
        load_rest.start()
        load_u.start()

        load_ang.wait()
        load_cls.wait()
        pack_fibers()
        load_row.wait()
        for side in range(2):
            source = jnp.broadcast_to(irow[side, 0].astype(F32), (CY, CY)).T
            spot = lax.broadcasted_iota(jnp.int32, (CY, CY), 1).astype(F32)
            rperm[side] = jnp.where(source == spot, 1.0, 0.0).astype(BF16)
        load_rest.wait()

        def weight_plane(x, carry):
            rows = rows_of(x)
            relax = 0.06 / inp[6, rows]
            inp[6, rows] = relax
            drive = relax * inp[7, rows]
            for k, value in enumerate(fiber_of(x)):
                fib[k, rows] = drive * value
                inp[3 + k, rows] = relax * inp[3 + k, rows]
            return carry

        lax.fori_loop(0, CX, weight_plane, 0)
        load_u.wait()
        pack_rows(0, 3)
        pack_corners(0, 3, 0)
        pack_corners(0, 3, 1)

        pl.semaphore_wait(barrier, 5)
        first_halo = halo_copies(0, 3)
        stiff = (
            remote(sec_ref.at[6, pl.ds(0, CY)], kx.at[1], STIFF_LEFT, near[STIFF_LEFT]),
            remote(sec_ref.at[6, pl.ds(COLS - CY, CY)], kx.at[0], STIFF_RIGHT, near[STIFF_RIGHT]),
        )
        for copy in (*first_halo, *stiff):
            copy.start()

        def halo_rows(phase):
            for side, sign in ((1, 0.5), (0, -0.5)):
                k = 3 * side
                at = 4 * (1 - side)
                hal[at] = halo_row(phase, k) + sign * halo_diff(phase, k + 1)
                hal[at + 1] = 3.0 * halo_row(phase, k + 1) + sign * halo_diff(phase, k)
                hal[at + 2] = halo_row(phase, k + 1)
                hal[at + 3] = halo_row(phase, k + 2)

        def relaxed(phase, x):
            here = ext[phase]
            mid, p, m = rows_of(x + 1), rows_of(x + 2), rows_of(x)
            c0, c1, c2 = here[0, mid], here[1, mid], here[2, mid]
            p0, p1, p2 = here[0, p], here[1, p], here[2, p]
            m0, m1, m2 = here[0, m], here[1, m], here[2, m]
            d0, d1, d2 = 0.5 * (p0 - m0), 0.5 * (p1 - m1), 0.5 * (p2 - m2)
            y2u, y2d = y_up(c2, row_at(3, x)), y_down(c2, row_at(7, x))
            e1 = 0.5 * (y_up(c1, row_at(2, x)) - y_down(c1, row_at(6, x)))
            e2 = 0.5 * (y2u - y2d)
            t1, t2 = 3.0 * c1, 3.0 * c2
            cross = d0 + e1
            s0 = (3.0 * (p0 + m0) + (y_up(c0 + d1, row_at(0, x)) + y_down(c0 - d1, row_at(4, x)))
                  + (z_up(c0 + d2) + z_down(c0 - d2)))
            s1 = ((p1 + m1) + (y_up(t1 + d0, row_at(1, x)) + y_down(t1 - d0, row_at(5, x)))
                  + (z_up(c1 + e2) + z_down(c1 - e2)))
            s2 = (p2 + m2) + (y2u + y2d) + (z_up(t2 + cross) + z_down(t2 - cross))
            return 0.4 * c0 + 0.06 * s0, 0.4 * c1 + 0.06 * s1, 0.4 * c2 + 0.06 * s2

        def tie_forces(phase, side):
            here = ext[phase]
            far = pl.ds((0, TOP)[side], CY)
            pieces = []
            for k in range(3):
                pieces += list(split3((2.0 * kx[side]) * here[k, far]))
            got = jnp.dot(rperm[side], jnp.concatenate(pieces, axis=1), preferred_element_type=F32)
            x = ENDS[side]
            relax = inp[6, rows_of(x)]
            result = []
            for k in range(3):
                at = 3 * NZ * k
                picked = got[:, at:at + NZ] + (got[:, at + NZ:at + 2 * NZ] + got[:, at + 2 * NZ:at + 3 * NZ])
                result.append(relax * picked - 0.12 * here[k, rows_of(x + 1)])
            return result

        def receive(slot, ref):
            remote(ref, ref, slot, partner).wait_recv()

        def base_plane(x, carry):
            rows = rows_of(x)
            for k, value in enumerate(relaxed(0, x)):
                base[k, rows] = value + inp[3 + k, rows]
            return carry

        def activate_plane(x, carry):
            rows = rows_of(x)
            tension = tbuf[rows]
            out_ref[3, rows] = inp[7, rows] * tension
            for k in range(3):
                ext1[k, rows_of(x + 1)] = base[k, rows] + fib[k, rows] * tension
            return carry

        def last_plane(x, carry):
            rows = rows_of(x)
            tension = tbuf[rows]
            for k, value in enumerate(relaxed(1, x)):
                out_ref[k, rows] = value + inp[3 + k, rows] + fib[k, rows] * tension
            return carry

        first_halo[ACROSS].wait_recv()
        halo_rows(0)
        lax.fori_loop(1, CX - 1, base_plane, 0)
        second_halo = halo_copies(1, 3)
        for side, slot in ((1, TEN_LAST), (0, TEN_FIRST)):
            x = ENDS[side]
            wait_side(first_halo, side)
            stiff[1 - side].wait_recv()
            unpack_corners(0, 3, side)
            halo_rows(0)
            base_plane(x, 0)
            for k, value in enumerate(tie_forces(0, side)):
                base[k, rows_of(x)] += value
            receive(slot, tbuf.at[rows_of(x)])
            activate_plane(x, 0)
            pack_corners(1, 3, side)
            second_halo[side].start()
            second_halo[DIAG_LEFT + side].start()
        receive(TEN_ROWS, trow)
        for side, y in ((0, CY - 1), (1, 0)):
            for k in range(3):
                own = pl.ds(y, CX, stride=CY)
                ypk[1, 3 * side + k] = base[k, own] + fib[k, own] * trow[side]
        second_halo[ACROSS].start()

        for index, ((low, high), ready) in enumerate(CHUNKS):
            rows = rows_of(low, high - low)
            receive(TEN_BULK + index, tbuf.at[rows])
            lax.fori_loop(low, high, activate_plane, 0)
            if index == 0:
                second_halo[ACROSS].wait_recv()
                halo_rows(1)
            lax.fori_loop(*ready, last_plane, 0)
        last_plane(CX - 2, 0)
        for side in (1, 0):
            x = ENDS[side]
            wait_side(second_halo, side)
            unpack_corners(1, 3, side)
            halo_rows(1)
            last_plane(x, 0)
            for k, value in enumerate(tie_forces(1, side)):
                out_ref[k, rows_of(x)] += value
        for copy in (*first_halo, *second_halo, *stiff):
            copy.wait_send()


def solution(mesh):
    n_gx = mesh.shape["gx"]

    def local(sections, fiber_angles, fiber_class, row_map, interface_rows):
        vmem = pltpu.VMEM
        field, padded = (COLS, NZ), (EXT, NZ)
        out = pl.pallas_call(
            functools.partial(kernel, n_gx),
            out_shape=jax.ShapeDtypeStruct((4, COLS, NZ), F32),
            in_specs=[pl.BlockSpec(memory_space=pltpu.HBM)] * 5,
            out_specs=pl.BlockSpec(memory_space=pltpu.VMEM),
            scratch_shapes=[
                vmem((8, *field), F32),
                vmem((3, *padded), F32),
                vmem((3, *padded), F32),
                vmem((3, *field), F32),
                vmem((3, *field), F32),
                vmem((3, CY, NZ), F32),
                vmem(field, F32),
                vmem((2, CX, NZ), F32),
                vmem((COLS, COLS), BF16),
                vmem((COLS, 3 * NZ), BF16),
                vmem((2, CY, CY), BF16),
                vmem((2, 3, CY, NZ), F32),
                vmem((2, 6, 32, NZ), F32),
                vmem((2, 6, CX, NZ), F32),
                vmem((2, 2, 8, NZ), F32),
                vmem((2, 2, 8, NZ), F32),
                vmem((8, CX, NZ), F32),
                vmem((2, CY, NZ), F32),
                vmem((2, CLASSES), F32),
                vmem((CX * 8, CY), jnp.int32),
                vmem((1, 1, COLS), jnp.int32),
                vmem((2, 1, 1, CY), jnp.int32),
                pltpu.SemaphoreType.DMA((11,)),
                pltpu.SemaphoreType.DMA((N_COPIES,)),
                pltpu.SemaphoreType.DMA((N_COPIES,)),
            ],
            compiler_params=pltpu.CompilerParams(
                collective_id=0, has_side_effects=True, vmem_limit_bytes=24 * 1024 * 1024),
        )(*[pltpu.with_memory_space_constraint(operand, pltpu.HBM) for operand in (
            sections.reshape(8, COLS, NZ), fiber_angles.T, fiber_class.transpose(0, 2, 1).reshape(CX * 8, CY), row_map,
            interface_rows)])
        return out.reshape(1, 4, CX, CY, NZ)

    in_specs = (
        P("sec", None, "gx", "gy", None),
        P(),
        P("gx", "gy", None),
        P("gx", "gy", None),
        P(None, "gx", "gy", None),
    )
    out_specs = P("sec", None, "gx", "gy", None)
    return jax.shard_map(local, mesh=mesh, in_specs=in_specs, out_specs=out_specs, check_vma=False)
```

time: 35.9 us -> 27 us (0.75)
  local copies, waits for them, and re-layouts: 5.63 us -> 0.97 us
  Pallas kernels: 30 us -> 25.9 us
    unnamed x9 -> x1, local copies, waits for them, and re-layouts: 5.63 us -> 0.97 us
    pallas_call x1, Pallas kernels: 30 us -> 25.9 us  [local(): pl.pallas_call(functools.partial(kernel, n_gx), out_shape=jax.ShapeDtypeS...]
where the time goes in v2:
time: 27 us; the launch traced here: 26.8 us
  Pallas kernels  25.9 us (96%)
  local copies, waits for them, and re-layouts  0.97 us (4%)
    pallas_call x1, Pallas kernels, local(): pl.pallas_call(functools.partial(kernel, n_gx), out_shape=jax.ShapeDtypeS...  25.9 us
    unnamed x1, local copies, waits for them, and re-layouts  0.97 us

profile of v2, /device:TPU:2, one launch (start us, length us, event | category | flops | bytes accessed | tf_op | source)
XLA Modules:
  0.0 26.8 jit_solution(6314277277374993751)
XLA Ops:
  0.0 25.9 %shard_map.55 = f32[4,512,128]{2,1,0:T(8,128)S(1)} custom-call(f32[8,512,128]{2,1,0:T(8,128)} %bitcast.7, f32[2,8]{1,0:T(2,128)} %bitcast.9, s32[128,32]{1,0:T(8,128)} %bitcast.8, s32[1,1,512]{2,1,0:T(1,128)} %rmap_ref.1, s32[2,1,1,32]{3,2,1,0:T(1,128)} %irow_ref.1), custom_call_target="tpu_custom_call" | custom-call | tf_op jit(solution)/shard_map/pallas_call | solution.py:501
  25.9 1.0 %copy.7 = f32[1,4,16,32,128]{4,3,2,1,0:T(8,128)} copy(f32[1,4,16,32,128]{4,3,2,1,0:T(8,128)S(1)} %bitcast.6) | data formatting | bytes 2097152

commit v3 on v2

v3 whole, which is shorter than its diff:
```python
import functools

import jax
import jax.numpy as jnp
from jax import lax
from jax.experimental import pallas as pl
from jax.experimental.pallas import tpu as pltpu
from jax.sharding import PartitionSpec as P

MESH = pl.DeviceIdType.MESH
F32, BF16 = jnp.float32, jnp.bfloat16

CX, CY, NZ = 16, 32, 128
COLS = CX * CY
TOP = COLS + CY
EXT = COLS + 2 * CY
CLASSES = 8
DT = 0.1

CHUNKS = (((1, 5), (2, 4)), ((5, 9), (4, 8)), ((9, 13), (8, 12)), ((13, 15), (12, 14)))

LEFT, RIGHT, ACROSS, DIAG_LEFT, DIAG_RIGHT, STIFF_LEFT, STIFF_RIGHT = range(7)
ACROSS_FIRST, ACROSS_LAST = 5, 6
EDGE_LEFT, EDGE_RIGHT = 5, 6
TEN_FIRST, TEN_LAST, TEN_ROWS, TEN_BULK = 16, 17, 18, 19
N_COPIES = TEN_BULK + len(CHUNKS)
ENDS = (0, CX - 1)


def rows_of(x, count=1):
    if isinstance(x, int):
        return pl.ds(x * CY, count * CY)
    return pl.ds(pl.multiple_of(x * CY, CY), count * CY)


def lanes(count=CY):
    return lax.broadcasted_iota(jnp.int32, (count, NZ), 1)


def sublanes():
    return lax.broadcasted_iota(jnp.int32, (CY, NZ), 0)


def z_up(a):
    return jnp.where(lanes(a.shape[0]) == NZ - 1, 0.0, pltpu.roll(a, NZ - 1, 1))


def z_down(a):
    return jnp.where(lanes(a.shape[0]) == 0, 0.0, pltpu.roll(a, 1, 1))


def y_up(a, row):
    moved = pltpu.roll(a, CY - 1, 0)
    return moved if row is None else jnp.where(sublanes() == CY - 1, jnp.broadcast_to(row, (CY, NZ)), moved)


def y_down(a, row):
    moved = pltpu.roll(a, 1, 0)
    return moved if row is None else jnp.where(sublanes() == 0, jnp.broadcast_to(row, (CY, NZ)), moved)


def sig(v):
    return 1.0 / (1.0 + jnp.exp(-v))


def split3(a):
    high = a.astype(BF16)
    rest = a - high.astype(F32)
    mid = rest.astype(BF16)
    low = (rest - mid.astype(F32)).astype(BF16)
    return high, mid, low


def kernel(n_gx, sec_ref, ang_ref, cls_ref, rmap_ref, irow_ref, out_ref,
           inp, ext0, ext1, fib, base, rel, tbl, clsx, tbuf, trow, perm, parts, rperm, tie,
           halo, ypk, corner_out, corner_in, edge_out, edge_in, hal, kx, ang, cls, rmap, irow,
           load_sem, send_sem, recv_sem):
    sec, gx, gy = lax.axis_index("sec"), lax.axis_index("gx"), lax.axis_index("gy")
    left, right = lax.rem(gx + n_gx - 1, n_gx), lax.rem(gx + 1, n_gx)
    across = 1 - gy
    near = {
        LEFT: (sec, left, gy), RIGHT: (sec, right, gy), ACROSS: (sec, gx, across),
        DIAG_LEFT: (sec, left, across), DIAG_RIGHT: (sec, right, across),
    }
    near[STIFF_LEFT], near[STIFF_RIGHT] = near[LEFT], near[RIGHT]
    partner = (1 - sec, gx, gy)
    ext = (ext0, ext1)

    barrier = pltpu.get_barrier_semaphore()
    for direction in (LEFT, RIGHT, ACROSS):
        pl.semaphore_signal(barrier, inc=1, device_id=near[direction], device_id_type=MESH)

    def load(src, dst, slot):
        return pltpu.make_async_copy(src, dst, load_sem.at[slot])

    def remote(src, dst, slot, device):
        return pltpu.make_async_remote_copy(
            src_ref=src, dst_ref=dst, send_sem=send_sem.at[slot], recv_sem=recv_sem.at[slot],
            device_id=device, device_id_type=MESH)

    def halo_copies(phase, fields):
        first, own = pl.ds(0, fields), ext[phase]
        low, high = own.at[first, pl.ds(CY, CY)], own.at[first, pl.ds(COLS, CY)]
        both = pl.ds(0, 2 * fields)
        slot = phase * 8
        copies = (
            remote(low, own.at[first, pl.ds(TOP, CY)], slot + LEFT, near[LEFT]),
            remote(high, own.at[first, pl.ds(0, CY)], slot + RIGHT, near[RIGHT]),
            remote(ypk.at[phase, both], halo.at[phase, both, pl.ds(8, CX)], slot + ACROSS, near[ACROSS]),
        )
        if phase == 1:
            copies += (
                remote(corner_out.at[0], corner_in.at[1], slot + DIAG_LEFT, near[DIAG_LEFT]),
                remote(corner_out.at[1], corner_in.at[0], slot + DIAG_RIGHT, near[DIAG_RIGHT]),
                remote(corner_out.at[0], corner_in.at[2], slot + ACROSS_FIRST, near[ACROSS]),
                remote(corner_out.at[1], corner_in.at[3], slot + ACROSS_LAST, near[ACROSS]),
            )
        return copies

    def plane_row(part, side):
        return CY + ENDS[side] * CY + (CY - 1, 0)[part]

    def far_row(part, side):
        return (0, TOP)[side] + (CY - 1, 0)[part]

    def pack_corners(fields, raw, side):
        for part in range(2):
            row = plane_row(part, side)
            for k in range(fields):
                at = part * fields + k
                corner_out[side, at:at + 1] = ext1[k, row:row + 1]
            for k in range(raw):
                at = 2 * fields + part * raw + k
                corner_out[side, at:at + 1] = ext0[k, row:row + 1]

    def pack_rows(phase, fields):
        for field in range(fields):
            ypk[phase, field] = ext[phase][field, pl.ds(CY + CY - 1, CX, stride=CY)]
            ypk[phase, fields + field] = ext[phase][field, pl.ds(CY, CX, stride=CY)]

    def wait_side(copies, side):
        copies[1 - side].wait_recv()
        if len(copies) > 3:
            copies[DIAG_RIGHT - side].wait_recv()
            copies[ACROSS_FIRST + side].wait_recv()

    def start_side(copies, side):
        copies[side].start()
        if len(copies) > 3:
            copies[DIAG_LEFT + side].start()
            copies[ACROSS_FIRST + side].start()

    def finish_side(fields, side, added):
        sign = (-1.0, 1.0)[side]
        for part in range(2):
            opposite = 1 - part
            own, far = plane_row(part, side), far_row(part, side)
            row, corner = (8, 7 + CX)[side], (7, 8 + CX)[side]
            signed = sign * (1.0, -1.0)[part]

            def across_old(k, part=part):
                at = (1 - part) * fields + k
                return halo[0, at, row:row + 1]

            def diag_old(k, part=part):
                return corner_in[side, added.raw_at(1 - part, k):added.raw_at(1 - part, k) + 1]

            def own_old(k, part=part):
                at = plane_row(1 - part, side)
                return ext0[k, at:at + 1]

            def far_old(k, part=part):
                at = far_row(1 - part, side)
                return ext0[k, at:at + 1]

            for k in range(fields):
                at = part * fields + k
                if k < 2:
                    ext1[k, own:own + 1] += signed * added(k, "own", part, side, diag_old)
                    ext1[k, far:far + 1] -= signed * added(k, "far", part, side, across_old)
                halo[1, at, corner:corner + 1] = (
                    corner_in[side, at:at + 1] - signed * added(k, "diag", part, side, own_old))
                halo[1, at, row:row + 1] = (
                    corner_in[2 + side, at:at + 1] + signed * added(k, "across", part, side, far_old))

    for k in range(6):
        for row in (7, 8 + CX):
            halo[0, k, row:row + 1] = jnp.zeros((1, NZ), F32)

    def halo_row(phase, k):
        return halo[phase, k, 8:8 + CX]

    def halo_diff(phase, k):
        return halo[phase, k, 9:9 + CX] - halo[phase, k, 7:7 + CX]

    def row_at(k, x, inner):
        return None if inner else hal[k, pl.ds(x, 1)]

    def row_set(phase, fields, y):
        sets = []
        for at in (y, y + 1, y - 1):
            if at in (-1, CY):
                first = fields if at == CY else 0
                rows = [halo[phase, first + field, 8:8 + CX] for field in range(fields)]
            else:
                rows = [ext[phase][field, pl.ds(CY + at, CX, stride=CY)] for field in range(fields)]
            sets.append([(row, pltpu.roll(row, CX - 1, 0), pltpu.roll(row, 1, 0)) for row in rows])
        return sets

    def spread_fibers():
        azimuth, elevation = ang[0:1, :], ang[1:2, :]
        flat = jnp.cos(elevation)
        for k, value in enumerate((jnp.cos(azimuth) * flat, jnp.sin(azimuth) * flat, jnp.sin(elevation))):
            for c in range(CLASSES):
                tbl[k, c:c + 1] = jnp.broadcast_to(value[:, c:c + 1], (1, NZ))
        kind = cls[...].astype(F32).T.astype(BF16)
        from_lane = lax.broadcasted_iota(jnp.int32, (NZ, CX * NZ), 0)
        to_lane = lax.broadcasted_iota(jnp.int32, (NZ, CX * NZ), 1) // 16
        spread = jnp.where(from_lane == to_lane, 1.0, 0.0).astype(BF16)
        wide = jnp.dot(kind, spread, preferred_element_type=F32)
        for x in range(CX):
            clsx[x * CY:(x + 1) * CY] = wide[:, x * NZ:(x + 1) * NZ]

    def fiber_of(x):
        kind = clsx[rows_of(x)]
        bit2 = kind >= 3.5
        kind = jnp.where(bit2, kind - 4.0, kind)
        bit1 = kind >= 1.5
        bit0 = jnp.where(bit1, kind - 2.0, kind) >= 0.5
        fields = []
        for k in range(3):
            pick = [jnp.broadcast_to(tbl[k, c:c + 1], (CY, NZ)) for c in range(CLASSES)]
            pick = [jnp.where(bit0, pick[2 * c + 1], pick[2 * c]) for c in range(4)]
            pick = [jnp.where(bit1, pick[2 * c + 1], pick[2 * c]) for c in range(2)]
            fields.append(jnp.where(bit2, pick[1], pick[0]))
        return fields


    @pl.when(sec == 0)
    def _():
        loads = [load(sec_ref.at[0], ext0.at[0, pl.ds(CY, COLS)], 0)]
        loads += [load(sec_ref.at[k], inp.at[k], k) for k in range(1, 8)]
        load_map = load(rmap_ref, rmap, 8)
        load_cls = load(cls_ref, cls, 9)
        load_ang = load(ang_ref, ang, 10)
        load_map.start()
        for k in (0, 1, 2, 3, 6, 7):
            loads[k].start()
        load_cls.start()
        load_ang.start()
        loads[4].start()
        loads[5].start()

        load_map.wait()
        source = jnp.broadcast_to(rmap[0].astype(F32), (8, COLS)).T[:, 0:1]
        spot = lax.broadcasted_iota(jnp.int32, (COLS, COLS), 1).astype(F32)
        perm[...] = jnp.where(jnp.broadcast_to(source, (COLS, COLS)) == spot, 1.0, 0.0).astype(BF16)

        for k in (0, 1, 2, 3, 6, 7):
            loads[k].wait()

        def tension_plane(x, carry):
            rows = rows_of(x)
            v = ext0[0, rows_of(x + 1)]
            c, d, f, b, s = inp[1, rows], inp[2, rows], inp[3, rows], inp[6, rows], inp[7, rows]
            square = c * c
            q = square / (square + 0.25)
            flow = 1.2 * d * f * (v - 2.0)
            binding = 2.0 * c * (1.0 - b) - 0.4 * b
            c = c + DT * (-0.3 * flow - 0.5 * c - binding)
            base[0, rows] = c
            base[1, rows] = q
            base[2, rows] = flow
            inp[6, rows] = b + DT * binding
            s = s + DT * (q - s) / 2.0
            square = c * c
            q = square / (square + 0.25)
            out_ref[1, rows] = q
            s = s + DT * (q - s) / 2.0
            out_ref[3, rows] = s
            for k, part in enumerate(split3(s)):
                parts[rows, k * NZ:(k + 1) * NZ] = part
            return carry

        lax.fori_loop(0, CX, tension_plane, 0)

        def permuted(low, high):
            moved = jnp.dot(perm[low * CY:high * CY], parts[...], preferred_element_type=F32)
            tbuf[low * CY:high * CY] = moved[:, 0:NZ] + (moved[:, NZ:2 * NZ] + moved[:, 2 * NZ:])

        permuted(CX - 1, CX)
        permuted(0, CX - 1)
        trow[0] = tbuf[pl.ds(CY - 1, CX, stride=CY)]
        trow[1] = tbuf[pl.ds(0, CX, stride=CY)]
        pack_rows(0, 1)
        pl.semaphore_wait(barrier, 4)
        first_halo = halo_copies(0, 1)
        tension = [
            remote(tbuf.at[rows_of(CX - 1)], tbuf.at[rows_of(CX - 1)], TEN_LAST, partner),
            remote(trow, trow, TEN_ROWS, partner),
            remote(tbuf.at[rows_of(0)], tbuf.at[rows_of(0)], TEN_FIRST, partner),
        ]
        tension[0].start()
        first_halo[ACROSS].start()
        start_side(first_halo, 0)
        start_side(first_halo, 1)
        for k, ((low, high), _) in enumerate(CHUNKS):
            rows = rows_of(low, high - low)
            tension.append(remote(tbuf.at[rows], tbuf.at[rows], TEN_BULK + k, partner))
        for copy in tension[1:]:
            copy.start()
        loads[4].wait()
        loads[5].wait()

        def first_ions(x, carry):
            rows = rows_of(x)
            v = ext0[0, rows_of(x + 1)]
            d, f, n, r = inp[2, rows], inp[3, rows], inp[4, rows], inp[5, rows]
            flow, q = base[2, rows], base[1, rows]
            current = flow + 0.8 * n * (v + 1.0) + 0.6 * q * r * (v + 1.0) + 0.1 * v
            base[1, rows] = v - DT * current
            inp[2, rows] = d + DT * (sig(2.0 * v + 1.0) - d) / 0.5
            inp[3, rows] = f + DT * (sig(-2.0 * v) - f) / 3.0
            inp[4, rows] = n + DT * (sig(2.0 * v) - n)
            inp[5, rows] = r + DT * (sig(v - 0.5) - r) / 5.0
            return carry

        lax.fori_loop(0, CX, first_ions, 0)

        load_ang.wait()
        load_cls.wait()
        spread_fibers()

        def fiber_plane(x, carry):
            for k, value in enumerate(fiber_of(x)):
                fib[k, rows_of(x)] = value
            return carry

        lax.fori_loop(0, CX, fiber_plane, 0)
        for side in range(2):
            for part in range(2):
                row = plane_row(part, side) - CY
                factor = (0.375 * DT) * fib[0, row:row + 1] * fib[1, row:row + 1]
                edge_out[side, part:part + 1] = factor
                corner_out[side, 4 + part:5 + part] = factor
        edges = (
            remote(edge_out.at[0], edge_in.at[1], EDGE_LEFT, near[LEFT]),
            remote(edge_out.at[1], edge_in.at[0], EDGE_RIGHT, near[RIGHT]),
        )
        for copy in edges:
            copy.start()

        def added(k, where, part, side, old):
            if where == "own":
                factor = edge_out[side, part:part + 1]
            elif where == "far":
                factor = edge_in[side, part:part + 1]
            else:
                factor = corner_in[side + (2 if where == "across" else 0), 4 + part:5 + part]
            return factor * old(0)

        added.raw_at = lambda part, k: 2 + part

        def combined(fiber, c, v00, v11, v22, x01, x02, x12):
            f0, f1, f2 = fiber
            along = (f0 * (f0 * v00 + 0.5 * (f1 * x01 + f2 * x02))
                     + f1 * (f1 * v11 + 0.5 * (f2 * x12)) + f2 * f2 * v22)
            return 0.25 * (v00 + v11 + v22) + 0.75 * along

        def diffusion(phase, x, inner=False):
            here = ext[phase]
            c, p, m = here[0, rows_of(x + 1)], here[0, rows_of(x + 2)], here[0, rows_of(x)]
            d = p - m
            yu, yd = y_up(c, row_at(0, x, inner)), y_down(c, row_at(1, x, inner))
            e = yu - yd
            twice = 2.0 * c
            return combined(
                [fib[k, rows_of(x)] for k in range(3)], c, p + m - twice, yu + yd - twice, z_up(c) + z_down(c) - twice,
                y_up(d, row_at(2, x, inner)) - y_down(d, row_at(3, x, inner)), z_up(d) - z_down(d), z_up(e) - z_down(e))

        def diffusion_row(phase, y):
            ((c, p, m),), ((cu, pu, mu),), ((cd, pd, md),) = row_set(phase, 1, y)
            d, e, twice = p - m, cu - cd, 2.0 * c
            return combined(
                [fib[k, pl.ds(y, CX, stride=CY)] for k in range(3)], c, p + m - twice, cu + cd - twice,
                z_up(c) + z_down(c) - twice, (pu - mu) - (pd - md), z_up(d) - z_down(d), z_up(e) - z_down(e))

        def halo_rows(phase):
            hal[0] = halo_row(phase, 1)
            hal[1] = halo_row(phase, 0)
            hal[2] = halo_diff(phase, 1)
            hal[3] = halo_diff(phase, 0)

        def first_step(x, carry, inner=False):
            ext1[0, rows_of(x + 1)] = base[1, rows_of(x)] + DT * diffusion(0, x, inner)
            return carry

        lax.fori_loop(1, CX - 1, functools.partial(first_step, inner=True), 0)
        second_halo = halo_copies(1, 1)
        first_halo[ACROSS].wait_recv()
        for side, y in ((0, CY - 1), (1, 0)):
            row = base[1, pl.ds(y, CX, stride=CY)] + DT * diffusion_row(0, y)
            ypk[1, side] = row
            ext1[0, pl.ds(CY + y, CX, stride=CY)] = row
        second_halo[ACROSS].start()
        for side in (1, 0):
            wait_side(first_halo, side)
            halo_rows(0)
            first_step(ENDS[side], 0)
            pack_corners(1, 1, side)
            start_side(second_halo, side)

        def second_ions(x, carry):
            rows = rows_of(x)
            v, c, q = ext1[0, rows_of(x + 1)], base[0, rows], out_ref[1, rows]
            d, f, n, r, b = inp[2, rows], inp[3, rows], inp[4, rows], inp[5, rows], inp[6, rows]
            flow = 1.2 * d * f * (v - 2.0)
            current = flow + 0.8 * n * (v + 1.0) + 0.6 * q * r * (v + 1.0) + 0.1 * v
            binding = 2.0 * c * (1.0 - b) - 0.4 * b
            base[1, rows] = v - DT * current
            out_ref[1, rows] = c + DT * (-0.3 * flow - 0.5 * c - binding)
            out_ref[2, rows] = n + DT * (sig(2.0 * v) - n)
            return carry

        lax.fori_loop(1, CX - 1, second_ions, 0)

        def second_step(x, carry, inner=False):
            rows = rows_of(x)
            out_ref[0, rows] = base[1, rows] + DT * diffusion(1, x, inner)
            return carry

        lax.fori_loop(2, CX - 2, functools.partial(second_step, inner=True), 0)
        second_halo[ACROSS].wait_recv()
        for y in (CY - 1, 0):
            row = pl.ds(y, CX, stride=CY)
            out_ref[0, row] = base[1, row] + DT * diffusion_row(1, y)
        for side in (1, 0):
            wait_side(second_halo, side)
            edges[1 - side].wait_recv()
            second_halo[side].wait_send()
            finish_side(1, side, added)
            halo_rows(1)
            second_ions(ENDS[side], 0)
            second_step(ENDS[side], 0)
            second_step((1, CX - 2)[side], 0)
        for copy in (*first_halo, *second_halo[2:], *edges, *tension):
            copy.wait_send()


    @pl.when(sec == 1)
    def _():
        pl.semaphore_signal(barrier, inc=1, device_id=partner, device_id_type=MESH)
        load_u = load(sec_ref.at[pl.ds(0, 3)], ext0.at[:, pl.ds(CY, COLS)], 0)
        load_rest = load(sec_ref.at[pl.ds(3, 5)], inp.at[pl.ds(3, 5)], 1)
        load_row = load(irow_ref, irow, 8)
        load_cls = load(cls_ref, cls, 9)
        load_ang = load(ang_ref, ang, 10)
        load_u.start()
        load_ang.start()
        load_cls.start()
        load_row.start()
        load_rest.start()

        load_u.wait()
        pack_rows(0, 3)
        load_rest.wait()
        pl.semaphore_wait(barrier, 3)
        first_halo = halo_copies(0, 3)
        stiff = (
            remote(inp.at[6, pl.ds(0, CY)], kx.at[1], STIFF_LEFT, near[STIFF_LEFT]),
            remote(inp.at[6, pl.ds(COLS - CY, CY)], kx.at[0], STIFF_RIGHT, near[STIFF_RIGHT]),
        )
        first_halo[ACROSS].start()
        for side in range(2):
            start_side(first_halo, side)
            stiff[side].start()

        load_ang.wait()
        load_cls.wait()
        spread_fibers()
        load_row.wait()
        for side in range(2):
            source = jnp.broadcast_to(irow[side, 0].astype(F32), (CY, CY)).T
            spot = lax.broadcasted_iota(jnp.int32, (CY, CY), 1).astype(F32)
            rperm[side] = jnp.where(source == spot, 1.0, 0.0).astype(BF16)

        def weight_plane(x, carry):
            rows = rows_of(x)
            relax = 0.06 / inp[6, rows]
            rel[rows] = relax
            drive = relax * inp[7, rows]
            for k, value in enumerate(fiber_of(x)):
                fib[k, rows] = drive * value
                inp[3 + k, rows] = relax * inp[3 + k, rows]
            return carry

        lax.fori_loop(0, CX, weight_plane, 0)

        def halo_rows(phase):
            for side, sign in ((1, 0.5), (0, -0.5)):
                k = 3 * side
                at = 4 * (1 - side)
                hal[at] = halo_row(phase, k) + sign * halo_diff(phase, k + 1)
                hal[at + 1] = 3.0 * halo_row(phase, k + 1) + sign * halo_diff(phase, k)
                hal[at + 2] = halo_row(phase, k + 1)
                hal[at + 3] = halo_row(phase, k + 2)

        def relaxed(phase, x, inner):
            here = ext[phase]
            mid, p, m = rows_of(x + 1), rows_of(x + 2), rows_of(x)
            c0, c1, c2 = here[0, mid], here[1, mid], here[2, mid]
            p0, p1, p2 = here[0, p], here[1, p], here[2, p]
            m0, m1, m2 = here[0, m], here[1, m], here[2, m]
            row = [row_at(k, x, inner) for k in range(8)]
            d0, d1, d2 = 0.5 * (p0 - m0), 0.5 * (p1 - m1), 0.5 * (p2 - m2)
            y2u, y2d = y_up(c2, row[3]), y_down(c2, row[7])
            e1 = 0.5 * (y_up(c1, row[2]) - y_down(c1, row[6]))
            e2 = 0.5 * (y2u - y2d)
            t1, t2 = 3.0 * c1, 3.0 * c2
            cross = d0 + e1
            s0 = (3.0 * (p0 + m0) + (y_up(c0 + d1, row[0]) + y_down(c0 - d1, row[4]))
                  + (z_up(c0 + d2) + z_down(c0 - d2)))
            s1 = ((p1 + m1) + (y_up(t1 + d0, row[1]) + y_down(t1 - d0, row[5]))
                  + (z_up(c1 + e2) + z_down(c1 - e2)))
            s2 = (p2 + m2) + (y2u + y2d) + (z_up(t2 + cross) + z_down(t2 - cross))
            return 0.4 * c0 + 0.06 * s0, 0.4 * c1 + 0.06 * s1, 0.4 * c2 + 0.06 * s2

        def relaxed_row(phase, y):
            here, up, down = row_set(phase, 3, y)
            (c0, p0, m0), (c1, p1, m1), (c2, p2, m2) = here
            d0, d2 = 0.5 * (p0 - m0), 0.5 * (p2 - m2)
            u0, u1 = 0.5 * (up[0][1] - up[0][2]), 0.5 * (up[1][1] - up[1][2])
            b0, b1 = 0.5 * (down[0][1] - down[0][2]), 0.5 * (down[1][1] - down[1][2])
            e2 = 0.5 * (up[2][0] - down[2][0])
            cross = d0 + 0.5 * (up[1][0] - down[1][0])
            t2 = 3.0 * c2
            s0 = (3.0 * (p0 + m0) + ((up[0][0] + u1) + (down[0][0] - b1)) + (z_up(c0 + d2) + z_down(c0 - d2)))
            s1 = ((p1 + m1) + ((3.0 * up[1][0] + u0) + (3.0 * down[1][0] - b0)) + (z_up(c1 + e2) + z_down(c1 - e2)))
            s2 = (p2 + m2) + (up[2][0] + down[2][0]) + (z_up(t2 + cross) + z_down(t2 - cross))
            return 0.4 * c0 + 0.06 * s0, 0.4 * c1 + 0.06 * s1, 0.4 * c2 + 0.06 * s2

        def added(k, where, part, side, old):
            return 0.03 * old(1 - k) if k < 2 else 0.0

        added.raw_at = lambda part, k: 6 + 2 * part + k

        def tie_forces(phase, side):
            here = ext[phase]
            far = pl.ds((0, TOP)[side], CY)
            pieces = []
            for k in range(3):
                pieces += list(split3((2.0 * kx[side]) * here[k, far]))
            got = jnp.dot(rperm[side], jnp.concatenate(pieces, axis=1), preferred_element_type=F32)
            x = ENDS[side]
            relax = rel[rows_of(x)]
            result = []
            for k in range(3):
                at = 3 * NZ * k
                picked = got[:, at:at + NZ] + (got[:, at + NZ:at + 2 * NZ] + got[:, at + 2 * NZ:at + 3 * NZ])
                result.append(relax * picked - 0.12 * here[k, rows_of(x + 1)])
            return result

        def receive(slot, ref):
            remote(ref, ref, slot, partner).wait_recv()

        def base_plane(x, carry, inner=False):
            rows = rows_of(x)
            for k, value in enumerate(relaxed(0, x, inner)):
                base[k, rows] = value + inp[3 + k, rows]
            return carry

        def activate_plane(x, carry):
            rows = rows_of(x)
            tension = tbuf[rows]
            out_ref[3, rows] = inp[7, rows] * tension
            for k in range(3):
                ext1[k, rows_of(x + 1)] = base[k, rows] + fib[k, rows] * tension
            return carry

        def last_plane(x, carry, inner=False):
            rows = rows_of(x)
            tension = tbuf[rows]
            for k, value in enumerate(relaxed(1, x, inner)):
                out_ref[k, rows] = value + inp[3 + k, rows] + fib[k, rows] * tension
            return carry

        lax.fori_loop(1, CX - 1, functools.partial(base_plane, inner=True), 0)
        second_halo = halo_copies(1, 3)
        first_halo[ACROSS].wait_recv()
        receive(TEN_ROWS, trow)
        for side, y in ((0, CY - 1), (1, 0)):
            own = pl.ds(y, CX, stride=CY)
            for k, value in enumerate(relaxed_row(0, y)):
                value = value + inp[3 + k, own]
                base[k, own] = value
                ypk[1, 3 * side + k] = value + fib[k, own] * trow[side]
        second_halo[ACROSS].start()
        for side, slot in ((1, TEN_LAST), (0, TEN_FIRST)):
            x = ENDS[side]
            wait_side(first_halo, side)
            stiff[1 - side].wait_recv()
            halo_rows(0)
            base_plane(x, 0)
            for k, value in enumerate(tie_forces(0, side)):
                base[k, rows_of(x)] += value
            receive(slot, tbuf.at[rows_of(x)])
            activate_plane(x, 0)
            pack_corners(3, 2, side)
            start_side(second_halo, side)

        for index, ((low, high), ready_planes) in enumerate(CHUNKS):
            rows = rows_of(low, high - low)
            receive(TEN_BULK + index, tbuf.at[rows])
            lax.fori_loop(low, high, activate_plane, 0)
            lax.fori_loop(*ready_planes, functools.partial(last_plane, inner=True), 0)
        second_halo[ACROSS].wait_recv()
        for side, y in ((0, CY - 1), (1, 0)):
            own = pl.ds(y, CX, stride=CY)
            for k, value in enumerate(relaxed_row(1, y)):
                out_ref[k, own] = value + inp[3 + k, own] + fib[k, own] * trow[side]
        for side in (1, 0):
            x = ENDS[side]
            wait_side(second_halo, side)
            second_halo[side].wait_send()
            finish_side(3, side, added)
            halo_rows(1)
            last_plane((1, CX - 2)[side], 0)
            last_plane(x, 0)
            for k, value in enumerate(tie_forces(1, side)):
                out_ref[k, rows_of(x)] += value
        for copy in (*first_halo, *second_halo[2:], *stiff):
            copy.wait_send()


def solution(mesh):
    n_gx = mesh.shape["gx"]

    def local(sections, fiber_angles, fiber_class, row_map, interface_rows):
        vmem = pltpu.VMEM
        field, padded = (COLS, NZ), (EXT, NZ)
        out = pl.pallas_call(
            functools.partial(kernel, n_gx),
            out_shape=jax.ShapeDtypeStruct((4, COLS, NZ), F32),
            in_specs=[pl.BlockSpec(memory_space=pltpu.HBM)] * 5,
            out_specs=pl.BlockSpec(memory_space=pltpu.VMEM),
            scratch_shapes=[
                vmem((8, *field), F32),
                vmem((3, *padded), F32),
                vmem((3, *padded), F32),
                vmem((3, *field), F32),
                vmem((3, *field), F32),
                vmem(field, F32),
                vmem((3, CLASSES, NZ), F32),
                vmem(field, F32),
                vmem(field, F32),
                vmem((2, CX, NZ), F32),
                vmem((COLS, COLS), BF16),
                vmem((COLS, 3 * NZ), BF16),
                vmem((2, CY, CY), BF16),
                vmem((2, 3, CY, NZ), F32),
                vmem((2, 6, 32, NZ), F32),
                vmem((2, 6, CX, NZ), F32),
                vmem((2, 16, NZ), F32),
                vmem((4, 16, NZ), F32),
                vmem((2, 8, NZ), F32),
                vmem((2, 8, NZ), F32),
                vmem((8, CX, NZ), F32),
                vmem((2, CY, NZ), F32),
                vmem((2, CLASSES), F32),
                vmem((CX * 8, CY), jnp.int32),
                vmem((1, 1, COLS), jnp.int32),
                vmem((2, 1, 1, CY), jnp.int32),
                pltpu.SemaphoreType.DMA((11,)),
                pltpu.SemaphoreType.DMA((N_COPIES,)),
                pltpu.SemaphoreType.DMA((N_COPIES,)),
            ],
            compiler_params=pltpu.CompilerParams(
                collective_id=0, has_side_effects=True, vmem_limit_bytes=24 * 1024 * 1024),
        )(*[pltpu.with_memory_space_constraint(operand, pltpu.HBM) for operand in (
            sections.reshape(8, COLS, NZ), fiber_angles.T, fiber_class.transpose(0, 2, 1).reshape(CX * 8, CY), row_map,
            interface_rows)])
        return out.reshape(1, 4, CX, CY, NZ)

    in_specs = (
        P("sec", None, "gx", "gy", None),
        P(),
        P("gx", "gy", None),
        P("gx", "gy", None),
        P(None, "gx", "gy", None),
    )
    out_specs = P("sec", None, "gx", "gy", None)
    return jax.shard_map(local, mesh=mesh, in_specs=in_specs, out_specs=out_specs, check_vma=False)
```

time: 27 us -> 24.5 us (0.907)
  Pallas kernels: 25.9 us -> 23.4 us
    pallas_call x1, Pallas kernels: 25.9 us -> 23.4 us  [local(): pl.pallas_call(functools.partial(kernel, n_gx), out_shape=jax.ShapeDtypeS...]
where the time goes in v3:
time: 24.5 us; the launch traced here: 24.4 us
  Pallas kernels  23.4 us (96%)
  local copies, waits for them, and re-layouts  0.97 us (4%)
    pallas_call x1, Pallas kernels, local(): pl.pallas_call(functools.partial(kernel, n_gx), out_shape=jax.ShapeDtypeS...  23.4 us
    unnamed x1, local copies, waits for them, and re-layouts  0.97 us

profile of v3, /device:TPU:2, one launch (start us, length us, event | category | flops | bytes accessed | tf_op | source)
XLA Modules:
  0.0 24.4 jit_solution(6275500157532371712)
XLA Ops:
  0.0 23.4 %shard_map.55 = f32[4,512,128]{2,1,0:T(8,128)S(1)} custom-call(f32[8,512,128]{2,1,0:T(8,128)} %bitcast.7, f32[2,8]{1,0:T(2,128)} %bitcast.9, s32[128,32]{1,0:T(8,128)} %bitcast.8, s32[1,1,512]{2,1,0:T(1,128)} %rmap_ref.1, s32[2,1,1,32]{3,2,1,0:T(1,128)} %irow_ref.1), custom_call_target="tpu_custom_call" | custom-call | tf_op jit(solution)/shard_map/pallas_call | solution.py:641
  23.4 1.0 %copy.7 = f32[1,4,16,32,128]{4,3,2,1,0:T(8,128)} copy(f32[1,4,16,32,128]{4,3,2,1,0:T(8,128)S(1)} %bitcast.6) | data formatting | bytes 2097152

commit v4 on v3

--- a/solution.py
+++ b/solution.py
@@ -21,9 +21,11 @@
 
 LEFT, RIGHT, ACROSS, DIAG_LEFT, DIAG_RIGHT, STIFF_LEFT, STIFF_RIGHT = range(7)
 ACROSS_FIRST, ACROSS_LAST = 5, 6
-EDGE_LEFT, EDGE_RIGHT = 5, 6
+LIST_LEFT, LIST_RIGHT = 3, 4
+EDGE_LEFT, EDGE_RIGHT = 7, 15
 TEN_FIRST, TEN_LAST, TEN_ROWS, TEN_BULK = 16, 17, 18, 19
-N_COPIES = TEN_BULK + len(CHUNKS)
+SHARE_FIRST, SHARE_LAST = TEN_BULK + len(CHUNKS), TEN_BULK + len(CHUNKS) + 1
+N_COPIES = SHARE_LAST + 1
 ENDS = (0, CX - 1)
 
 
@@ -72,8 +74,9 @@
 
 
 def kernel(n_gx, sec_ref, ang_ref, cls_ref, rmap_ref, irow_ref, out_ref,
-           inp, ext0, ext1, fib, base, rel, tbl, clsx, tbuf, trow, perm, parts, rperm, tie,
+           inp, ext0, ext1, fib, base, rel, tbl, clsx, tbuf, trow, perm, parts, rperm,
            halo, ypk, corner_out, corner_in, edge_out, edge_in, hal, kx, ang, cls, rmap, irow,
+           far_irow, unfinished, share, share_out, share_in, end_out,
            load_sem, send_sem, recv_sem):
     sec, gx, gy = lax.axis_index("sec"), lax.axis_index("gx"), lax.axis_index("gy")
     left, right = lax.rem(gx + n_gx - 1, n_gx), lax.rem(gx + 1, n_gx)
@@ -101,6 +104,9 @@
     def halo_copies(phase, fields):
         first, own = pl.ds(0, fields), ext[phase]
         low, high = own.at[first, pl.ds(CY, CY)], own.at[first, pl.ds(COLS, CY)]
+        ends = corner_out
+        if phase == 1 and fields == 3:
+            low, high, ends = unfinished.at[0], unfinished.at[1], end_out
         both = pl.ds(0, 2 * fields)
         slot = phase * 8
         copies = (
@@ -112,8 +118,8 @@
             copies += (
                 remote(corner_out.at[0], corner_in.at[1], slot + DIAG_LEFT, near[DIAG_LEFT]),
                 remote(corner_out.at[1], corner_in.at[0], slot + DIAG_RIGHT, near[DIAG_RIGHT]),
-                remote(corner_out.at[0], corner_in.at[2], slot + ACROSS_FIRST, near[ACROSS]),
-                remote(corner_out.at[1], corner_in.at[3], slot + ACROSS_LAST, near[ACROSS]),
+                remote(ends.at[0], corner_in.at[2], slot + ACROSS_FIRST, near[ACROSS]),
+                remote(ends.at[1], corner_in.at[3], slot + ACROSS_LAST, near[ACROSS]),
             )
         return copies
 
@@ -123,15 +129,23 @@
     def far_row(part, side):
         return (0, TOP)[side] + (CY - 1, 0)[part]
 
-    def pack_corners(fields, raw, side):
+    def pack_corners(fields, side, into=corner_out):
         for part in range(2):
             row = plane_row(part, side)
             for k in range(fields):
                 at = part * fields + k
-                corner_out[side, at:at + 1] = ext1[k, row:row + 1]
-            for k in range(raw):
-                at = 2 * fields + part * raw + k
-                corner_out[side, at:at + 1] = ext0[k, row:row + 1]
+                into[side, at:at + 1] = ext1[k, row:row + 1]
+
+    def pack_edges(fields):
+        for side in range(2):
+            row = (8, 7 + CX)[side]
+            for k in range(2 * fields):
+                edge_out[side, k:k + 1] = halo[0, k, row:row + 1]
+
+    edges = (
+        remote(edge_out.at[0], edge_in.at[1], EDGE_LEFT, near[LEFT]),
+        remote(edge_out.at[1], edge_in.at[0], EDGE_RIGHT, near[RIGHT]),
+    )
 
     def pack_rows(phase, fields):
         for field in range(fields):
@@ -141,8 +155,9 @@
     def wait_side(copies, side):
         copies[1 - side].wait_recv()
         if len(copies) > 3:
-            copies[DIAG_RIGHT - side].wait_recv()
             copies[ACROSS_FIRST + side].wait_recv()
+            edges[1 - side].wait_recv()
+            copies[side].wait_send()
 
     def start_side(copies, side):
         copies[side].start()
@@ -152,40 +167,61 @@
 
     def finish_side(fields, side, added):
         sign = (-1.0, 1.0)[side]
+        row = (8, 7 + CX)[side]
         for part in range(2):
-            opposite = 1 - part
             own, far = plane_row(part, side), far_row(part, side)
-            row, corner = (8, 7 + CX)[side], (7, 8 + CX)[side]
             signed = sign * (1.0, -1.0)[part]
+
+            def diag_old(k, part=part):
+                at = (1 - part) * fields + k
+                return edge_in[side, at:at + 1]
 
             def across_old(k, part=part):
                 at = (1 - part) * fields + k
                 return halo[0, at, row:row + 1]
 
-            def diag_old(k, part=part):
-                return corner_in[side, added.raw_at(1 - part, k):added.raw_at(1 - part, k) + 1]
+            def far_old(k, part=part):
+                at = far_row(1 - part, side)
+                return ext0[k, at:at + 1]
+
+            for k in range(min(fields, 2)):
+                at = part * fields + k
+                ext1[k, own:own + 1] += signed * added(k, "own", part, side, diag_old)
+                if fields == 1:
+                    ext1[k, far:far + 1] -= signed * added(k, "far", part, side, across_old)
+                halo[1, at, row:row + 1] = (
+                    corner_in[2 + side, at:at + 1] + signed * added(k, "across", part, side, far_old))
+            if fields == 3:
+                at = part * fields + 2
+                halo[1, at, row:row + 1] = corner_in[2 + side, at:at + 1]
+
+    def add_corners(fields, side, added, copies):
+        copies[DIAG_RIGHT - side].wait_recv()
+        sign = (-1.0, 1.0)[side]
+        corner = []
+        for part in range(2):
+            signed = sign * (1.0, -1.0)[part]
 
             def own_old(k, part=part):
                 at = plane_row(1 - part, side)
                 return ext0[k, at:at + 1]
 
-            def far_old(k, part=part):
-                at = far_row(1 - part, side)
-                return ext0[k, at:at + 1]
-
-            for k in range(fields):
-                at = part * fields + k
-                if k < 2:
-                    ext1[k, own:own + 1] += signed * added(k, "own", part, side, diag_old)
-                    ext1[k, far:far + 1] -= signed * added(k, "far", part, side, across_old)
-                halo[1, at, corner:corner + 1] = (
-                    corner_in[side, at:at + 1] - signed * added(k, "diag", part, side, own_old))
-                halo[1, at, row:row + 1] = (
-                    corner_in[2 + side, at:at + 1] + signed * added(k, "across", part, side, far_old))
+            corner.append([corner_in[side, part * fields + k:part * fields + k + 1] for k in range(min(fields, 2))])
+            if fields == 1:
+                corner[part][0] -= signed * added(0, "diag", part, side, own_old)
+            else:
+                corner[part] = [value + share_in[side, 2 * part + k:2 * part + k + 1]
+                                for k, value in enumerate(corner[part])]
+        for part in range(2):
+            signed = sign * (1.0, -1.0)[part]
+            own = plane_row(part, side) - CY
+            for k in range(min(fields, 2)):
+                out_ref[k, own:own + 1] += signed * added(k, "own", part, side, lambda c, part=part: corner[1 - part][c])
 
     for k in range(6):
         for row in (7, 8 + CX):
             halo[0, k, row:row + 1] = jnp.zeros((1, NZ), F32)
+            halo[1, k, row:row + 1] = jnp.zeros((1, NZ), F32)
 
     def halo_row(phase, k):
         return halo[phase, k, 8:8 + CX]
@@ -341,25 +377,17 @@
             for part in range(2):
                 row = plane_row(part, side) - CY
                 factor = (0.375 * DT) * fib[0, row:row + 1] * fib[1, row:row + 1]
-                edge_out[side, part:part + 1] = factor
+                edge_out[side, 2 + part:3 + part] = factor
                 corner_out[side, 4 + part:5 + part] = factor
-        edges = (
-            remote(edge_out.at[0], edge_in.at[1], EDGE_LEFT, near[LEFT]),
-            remote(edge_out.at[1], edge_in.at[0], EDGE_RIGHT, near[RIGHT]),
-        )
-        for copy in edges:
-            copy.start()
 
         def added(k, where, part, side, old):
             if where == "own":
-                factor = edge_out[side, part:part + 1]
+                factor = edge_out[side, 2 + part:3 + part]
             elif where == "far":
-                factor = edge_in[side, part:part + 1]
+                factor = edge_in[side, 2 + part:3 + part]
             else:
                 factor = corner_in[side + (2 if where == "across" else 0), 4 + part:5 + part]
             return factor * old(0)
-
-        added.raw_at = lambda part, k: 2 + part
 
         def combined(fiber, c, v00, v11, v22, x01, x02, x12):
             f0, f1, f2 = fiber
@@ -398,6 +426,9 @@
         lax.fori_loop(1, CX - 1, functools.partial(first_step, inner=True), 0)
         second_halo = halo_copies(1, 1)
         first_halo[ACROSS].wait_recv()
+        pack_edges(1)
+        for copy in edges:
+            copy.start()
         for side, y in ((0, CY - 1), (1, 0)):
             row = base[1, pl.ds(y, CX, stride=CY)] + DT * diffusion_row(0, y)
             ypk[1, side] = row
@@ -407,7 +438,7 @@
             wait_side(first_halo, side)
             halo_rows(0)
             first_step(ENDS[side], 0)
-            pack_corners(1, 1, side)
+            pack_corners(1, side)
             start_side(second_halo, side)
 
         def second_ions(x, carry):
@@ -436,13 +467,12 @@
             out_ref[0, row] = base[1, row] + DT * diffusion_row(1, y)
         for side in (1, 0):
             wait_side(second_halo, side)
-            edges[1 - side].wait_recv()
-            second_halo[side].wait_send()
             finish_side(1, side, added)
             halo_rows(1)
             second_ions(ENDS[side], 0)
             second_step(ENDS[side], 0)
             second_step((1, CX - 2)[side], 0)
+            add_corners(1, side, added, second_halo)
         for copy in (*first_halo, *second_halo[2:], *edges, *tension):
             copy.wait_send()
 
@@ -464,25 +494,34 @@
         load_u.wait()
         pack_rows(0, 3)
         load_rest.wait()
+        load_row.wait()
         pl.semaphore_wait(barrier, 3)
         first_halo = halo_copies(0, 3)
         stiff = (
             remote(inp.at[6, pl.ds(0, CY)], kx.at[1], STIFF_LEFT, near[STIFF_LEFT]),
             remote(inp.at[6, pl.ds(COLS - CY, CY)], kx.at[0], STIFF_RIGHT, near[STIFF_RIGHT]),
         )
+        lists = (
+            remote(irow.at[0], far_irow.at[1], LIST_LEFT, near[LEFT]),
+            remote(irow.at[1], far_irow.at[0], LIST_RIGHT, near[RIGHT]),
+        )
         first_halo[ACROSS].start()
         for side in range(2):
             start_side(first_halo, side)
             stiff[side].start()
+            lists[side].start()
 
         load_ang.wait()
         load_cls.wait()
         spread_fibers()
-        load_row.wait()
+
+        def take_list(values, slot):
+            source = jnp.broadcast_to(values.astype(F32), (CY, CY)).T
+            spot = lax.broadcasted_iota(jnp.int32, (CY, CY), 1).astype(F32)
+            rperm[slot] = jnp.where(source == spot, 1.0, 0.0).astype(BF16)
+
         for side in range(2):
-            source = jnp.broadcast_to(irow[side, 0].astype(F32), (CY, CY)).T
-            spot = lax.broadcasted_iota(jnp.int32, (CY, CY), 1).astype(F32)
-            rperm[side] = jnp.where(source == spot, 1.0, 0.0).astype(BF16)
+            take_list(irow[side, 0], side)
 
         def weight_plane(x, carry):
             rows = rows_of(x)
@@ -505,12 +544,16 @@
                 hal[at + 2] = halo_row(phase, k + 1)
                 hal[at + 3] = halo_row(phase, k + 2)
 
-        def relaxed(phase, x, inner):
+        def relaxed(phase, x, inner, without=None):
             here = ext[phase]
             mid, p, m = rows_of(x + 1), rows_of(x + 2), rows_of(x)
             c0, c1, c2 = here[0, mid], here[1, mid], here[2, mid]
             p0, p1, p2 = here[0, p], here[1, p], here[2, p]
             m0, m1, m2 = here[0, m], here[1, m], here[2, m]
+            if without == 0:
+                m0 = m1 = m2 = jnp.zeros_like(c0)
+            if without == 1:
+                p0 = p1 = p2 = jnp.zeros_like(c0)
             row = [row_at(k, x, inner) for k in range(8)]
             d0, d1, d2 = 0.5 * (p0 - m0), 0.5 * (p1 - m1), 0.5 * (p2 - m2)
             y2u, y2d = y_up(c2, row[3]), y_down(c2, row[7])
@@ -542,23 +585,32 @@
         def added(k, where, part, side, old):
             return 0.03 * old(1 - k) if k < 2 else 0.0
 
-        added.raw_at = lambda part, k: 6 + 2 * part + k
+        def picked(slot, stiffness, planes):
+            pieces = []
+            for plane in planes:
+                pieces += list(split3((2.0 * stiffness) * plane))
+            got = jnp.dot(rperm[slot], jnp.concatenate(pieces, axis=1), preferred_element_type=F32)
+            return [got[:, at:at + NZ] + (got[:, at + NZ:at + 2 * NZ] + got[:, at + 2 * NZ:at + 3 * NZ])
+                    for at in (0, 3 * NZ, 6 * NZ)]
+
+        def far_plane(phase, side):
+            return [ext[phase][k, pl.ds((0, TOP)[side], CY)] for k in range(3)]
 
         def tie_forces(phase, side):
-            here = ext[phase]
-            far = pl.ds((0, TOP)[side], CY)
-            pieces = []
-            for k in range(3):
-                pieces += list(split3((2.0 * kx[side]) * here[k, far]))
-            got = jnp.dot(rperm[side], jnp.concatenate(pieces, axis=1), preferred_element_type=F32)
             x = ENDS[side]
             relax = rel[rows_of(x)]
-            result = []
-            for k in range(3):
-                at = 3 * NZ * k
-                picked = got[:, at:at + NZ] + (got[:, at + NZ:at + 2 * NZ] + got[:, at + 2 * NZ:at + 3 * NZ])
-                result.append(relax * picked - 0.12 * here[k, rows_of(x + 1)])
-            return result
+            got = picked(side, kx[side], far_plane(phase, side))
+            return [relax * got[k] - 0.12 * ext[phase][k, rows_of(x + 1)] for k in range(3)]
+
+        def contribution(planes, above, below, sign, relax, got):
+            p0, p1, p2 = planes
+            half = 0.5 * sign
+            across0 = half * (y_up(p0, above[0]) - y_down(p0, below[0]))
+            across1 = half * (y_up(p1, above[1]) - y_down(p1, below[1]))
+            s0 = 3.0 * p0 + across1 + half * (z_up(p2) - z_down(p2))
+            s1 = p1 + across0
+            s2 = p2 + half * (z_up(p0) - z_down(p0))
+            return [0.06 * value + relax * got[k] for k, value in enumerate((s0, s1, s2))]
 
         def receive(slot, ref):
             remote(ref, ref, slot, partner).wait_recv()
@@ -586,7 +638,59 @@
 
         lax.fori_loop(1, CX - 1, functools.partial(base_plane, inner=True), 0)
         second_halo = halo_copies(1, 3)
+        def send_end(side, slot):
+            x = ENDS[side]
+            rows = rows_of(x)
+            receive(slot, tbuf.at[rows])
+            tension = tbuf[rows]
+            out_ref[3, rows] = inp[7, rows] * tension
+            for k, value in enumerate(relaxed(0, x, False, without=side)):
+                value = value + inp[3 + k, rows] + fib[k, rows] * tension - 0.12 * ext0[k, rows_of(x + 1)]
+                unfinished[side, k] = value
+                for part, y in ((0, CY - 1), (1, 0)):
+                    at = 3 * part + k
+                    corner_out[side, at:at + 1] = value[y:y + 1]
+            second_halo[side].start()
+            second_halo[DIAG_LEFT + side].start()
+
+        nothing = jnp.zeros((1, NZ), F32)
+
+        def finish_end(side):
+            x = ENDS[side]
+            sign = (-1.0, 1.0)[side]
+            stiff[1 - side].wait_recv()
+            lists[1 - side].wait_recv()
+            take_list(far_irow[side, 0], 2 + side)
+            own = [ext0[k, rows_of(x + 1)] for k in range(3)]
+            row = (8, 7 + CX)[side]
+            below, above = ([halo[0, 3 * half + k, row:row + 1] for k in range(3)] for half in range(2))
+            got = picked(2 + side, inp[6, rows_of(x)], own)
+            for k, value in enumerate(contribution(own, above, below, -sign, 0.06 / kx[side], got)):
+                share[side, k] = value
+                for part, y in ((0, CY - 1), (1, 0)):
+                    if k < 2:
+                        share_out[side, 2 * part + k:2 * part + k + 1] = value[y:y + 1]
+            shares[side].start()
+            wait_side(first_halo, side)
+            far = far_plane(0, side)
+            got = picked(side, kx[side], far)
+            added_here = contribution(far, [nothing] * 3, [nothing] * 3, sign, rel[rows_of(x)], got)
+            for k, value in enumerate(added_here):
+                ext1[k, rows_of(x + 1)] = unfinished[side, k] + value
+            pack_corners(3, side, end_out)
+            second_halo[ACROSS_FIRST + side].start()
+
+        shares = (
+            remote(share_out.at[0], share_in.at[0], SHARE_FIRST, near[ACROSS]),
+            remote(share_out.at[1], share_in.at[1], SHARE_LAST, near[ACROSS]),
+        )
         first_halo[ACROSS].wait_recv()
+        halo_rows(0)
+        pack_edges(3)
+        for copy in edges:
+            copy.start()
+        send_end(1, TEN_LAST)
+        send_end(0, TEN_FIRST)
         receive(TEN_ROWS, trow)
         for side, y in ((0, CY - 1), (1, 0)):
             own = pl.ds(y, CX, stride=CY)
@@ -595,18 +699,8 @@
                 base[k, own] = value
                 ypk[1, 3 * side + k] = value + fib[k, own] * trow[side]
         second_halo[ACROSS].start()
-        for side, slot in ((1, TEN_LAST), (0, TEN_FIRST)):
-            x = ENDS[side]
-            wait_side(first_halo, side)
-            stiff[1 - side].wait_recv()
-            halo_rows(0)
-            base_plane(x, 0)
-            for k, value in enumerate(tie_forces(0, side)):
-                base[k, rows_of(x)] += value
-            receive(slot, tbuf.at[rows_of(x)])
-            activate_plane(x, 0)
-            pack_corners(3, 2, side)
-            start_side(second_halo, side)
+        for side in (1, 0):
+            finish_end(side)
 
         for index, ((low, high), ready_planes) in enumerate(CHUNKS):
             rows = rows_of(low, high - low)
@@ -620,15 +714,20 @@
                 out_ref[k, own] = value + inp[3 + k, own] + fib[k, own] * trow[side]
         for side in (1, 0):
             x = ENDS[side]
-            wait_side(second_halo, side)
-            second_halo[side].wait_send()
+            second_halo[1 - side].wait_recv()
+            for k in range(3):
+                ext1[k, pl.ds((0, TOP)[side], CY)] += share[side, k]
+            second_halo[ACROSS_FIRST + side].wait_recv()
+            edges[1 - side].wait_recv()
             finish_side(3, side, added)
             halo_rows(1)
             last_plane((1, CX - 2)[side], 0)
             last_plane(x, 0)
             for k, value in enumerate(tie_forces(1, side)):
                 out_ref[k, rows_of(x)] += value
-        for copy in (*first_halo, *second_halo[2:], *stiff):
+            shares[side].wait_recv()
+            add_corners(3, side, added, second_halo)
+        for copy in (*first_halo, *second_halo, *edges, *stiff, *lists, *shares):
             copy.wait_send()
 
 
@@ -656,12 +755,11 @@
                 vmem((2, CX, NZ), F32),
                 vmem((COLS, COLS), BF16),
                 vmem((COLS, 3 * NZ), BF16),
-                vmem((2, CY, CY), BF16),
-                vmem((2, 3, CY, NZ), F32),
+                vmem((4, CY, CY), BF16),
                 vmem((2, 6, 32, NZ), F32),
                 vmem((2, 6, CX, NZ), F32),
-                vmem((2, 16, NZ), F32),
-                vmem((4, 16, NZ), F32),
+                vmem((2, 8, NZ), F32),
+                vmem((4, 8, NZ), F32),
                 vmem((2, 8, NZ), F32),
                 vmem((2, 8, NZ), F32),
                 vmem((8, CX, NZ), F32),
@@ -670,6 +768,12 @@
                 vmem((CX * 8, CY), jnp.int32),
                 vmem((1, 1, COLS), jnp.int32),
                 vmem((2, 1, 1, CY), jnp.int32),
+                vmem((2, 1, 1, CY), jnp.int32),
+                vmem((2, 3, CY, NZ), F32),
+                vmem((2, 3, CY, NZ), F32),
+                vmem((2, 8, NZ), F32),
+                vmem((2, 8, NZ), F32),
+                vmem((2, 8, NZ), F32),
                 pltpu.SemaphoreType.DMA((11,)),
                 pltpu.SemaphoreType.DMA((N_COPIES,)),
                 pltpu.SemaphoreType.DMA((N_COPIES,)),

time: 24.5 us -> 22.9 us (0.935)
  the two profiles are of different devices: /device:TPU:2 before, /device:TPU:1 now
where the time goes in v4:
time: 22.9 us; the launch traced here: 22.8 us
  Pallas kernels  21.8 us (95%)
  local copies, waits for them, and re-layouts  0.97 us (4%)
    pallas_call x1, Pallas kernels, local(): pl.pallas_call(functools.partial(kernel, n_gx), out_shape=jax.ShapeDtypeS...  21.8 us
    unnamed x1, local copies, waits for them, and re-layouts  0.97 us

profile of v4, /device:TPU:1, one launch (start us, length us, event | category | flops | bytes accessed | tf_op | source)
XLA Modules:
  0.0 22.8 jit_solution(17840652075173860993)
XLA Ops:
  0.0 21.8 %shard_map.55 = f32[4,512,128]{2,1,0:T(8,128)S(1)} custom-call(f32[8,512,128]{2,1,0:T(8,128)} %bitcast.7, f32[2,8]{1,0:T(2,128)} %bitcast.9, s32[128,32]{1,0:T(8,128)} %bitcast.8, s32[1,1,512]{2,1,0:T(1,128)} %rmap_ref.1, s32[2,1,1,32]{3,2,1,0:T(1,128)} %irow_ref.1), custom_call_target="tpu_custom_call" | custom-call | tf_op jit(solution)/shard_map/pallas_call | solution.py:740
  21.8 1.0 %copy.7 = f32[1,4,16,32,128]{4,3,2,1,0:T(8,128)} copy(f32[1,4,16,32,128]{4,3,2,1,0:T(8,128)S(1)} %bitcast.6) | data formatting | bytes 2097152

commit v5 on v4

--- a/solution.py
+++ b/solution.py
@@ -154,10 +154,6 @@
 
     def wait_side(copies, side):
         copies[1 - side].wait_recv()
-        if len(copies) > 3:
-            copies[ACROSS_FIRST + side].wait_recv()
-            edges[1 - side].wait_recv()
-            copies[side].wait_send()
 
     def start_side(copies, side):
         copies[side].start()
@@ -169,17 +165,13 @@
         sign = (-1.0, 1.0)[side]
         row = (8, 7 + CX)[side]
         for part in range(2):
-            own, far = plane_row(part, side), far_row(part, side)
+            own = plane_row(part, side)
             signed = sign * (1.0, -1.0)[part]
 
             def diag_old(k, part=part):
                 at = (1 - part) * fields + k
                 return edge_in[side, at:at + 1]
 
-            def across_old(k, part=part):
-                at = (1 - part) * fields + k
-                return halo[0, at, row:row + 1]
-
             def far_old(k, part=part):
                 at = far_row(1 - part, side)
                 return ext0[k, at:at + 1]
@@ -187,13 +179,19 @@
             for k in range(min(fields, 2)):
                 at = part * fields + k
                 ext1[k, own:own + 1] += signed * added(k, "own", part, side, diag_old)
-                if fields == 1:
-                    ext1[k, far:far + 1] -= signed * added(k, "far", part, side, across_old)
                 halo[1, at, row:row + 1] = (
                     corner_in[2 + side, at:at + 1] + signed * added(k, "across", part, side, far_old))
             if fields == 3:
                 at = part * fields + 2
                 halo[1, at, row:row + 1] = corner_in[2 + side, at:at + 1]
+
+    def finish_far(side, added):
+        sign = (-1.0, 1.0)[side]
+        row = (8, 7 + CX)[side]
+        for part in range(2):
+            far = far_row(part, side)
+            old = halo[0, 1 - part, row:row + 1]
+            ext1[0, far:far + 1] -= sign * (1.0, -1.0)[part] * added(0, "far", part, side, lambda k, old=old: old)
 
     def add_corners(fields, side, added, copies):
         copies[DIAG_RIGHT - side].wait_recv()
@@ -280,10 +278,10 @@
         load_cls = load(cls_ref, cls, 9)
         load_ang = load(ang_ref, ang, 10)
         load_map.start()
+        load_cls.start()
+        load_ang.start()
         for k in (0, 1, 2, 3, 6, 7):
             loads[k].start()
-        load_cls.start()
-        load_ang.start()
         loads[4].start()
         loads[5].start()
 
@@ -291,6 +289,23 @@
         source = jnp.broadcast_to(rmap[0].astype(F32), (8, COLS)).T[:, 0:1]
         spot = lax.broadcasted_iota(jnp.int32, (COLS, COLS), 1).astype(F32)
         perm[...] = jnp.where(jnp.broadcast_to(source, (COLS, COLS)) == spot, 1.0, 0.0).astype(BF16)
+
+        load_ang.wait()
+        load_cls.wait()
+        spread_fibers()
+
+        def fiber_plane(x, carry):
+            for k, value in enumerate(fiber_of(x)):
+                fib[k, rows_of(x)] = value
+            return carry
+
+        lax.fori_loop(0, CX, fiber_plane, 0)
+        for side in range(2):
+            for part in range(2):
+                row = plane_row(part, side) - CY
+                factor = (0.375 * DT) * fib[0, row:row + 1] * fib[1, row:row + 1]
+                edge_out[side, 2 + part:3 + part] = factor
+                corner_out[side, 4 + part:5 + part] = factor
 
         for k in (0, 1, 2, 3, 6, 7):
             loads[k].wait()
@@ -363,23 +378,6 @@
 
         lax.fori_loop(0, CX, first_ions, 0)
 
-        load_ang.wait()
-        load_cls.wait()
-        spread_fibers()
-
-        def fiber_plane(x, carry):
-            for k, value in enumerate(fiber_of(x)):
-                fib[k, rows_of(x)] = value
-            return carry
-
-        lax.fori_loop(0, CX, fiber_plane, 0)
-        for side in range(2):
-            for part in range(2):
-                row = plane_row(part, side) - CY
-                factor = (0.375 * DT) * fib[0, row:row + 1] * fib[1, row:row + 1]
-                edge_out[side, 2 + part:3 + part] = factor
-                corner_out[side, 4 + part:5 + part] = factor
-
         def added(k, where, part, side, old):
             if where == "own":
                 factor = edge_out[side, 2 + part:3 + part]
@@ -429,17 +427,18 @@
         pack_edges(1)
         for copy in edges:
             copy.start()
-        for side, y in ((0, CY - 1), (1, 0)):
-            row = base[1, pl.ds(y, CX, stride=CY)] + DT * diffusion_row(0, y)
-            ypk[1, side] = row
-            ext1[0, pl.ds(CY + y, CX, stride=CY)] = row
-        second_halo[ACROSS].start()
+        halo_rows(0)
         for side in (1, 0):
             wait_side(first_halo, side)
-            halo_rows(0)
             first_step(ENDS[side], 0)
             pack_corners(1, side)
             start_side(second_halo, side)
+            if side == 1:
+                for part, y in ((0, CY - 1), (1, 0)):
+                    row = base[1, pl.ds(y, CX, stride=CY)] + DT * diffusion_row(0, y)
+                    ypk[1, part] = row
+                    ext1[0, pl.ds(2 * CY + y, CX - 2, stride=CY)] = row[1:CX - 1]
+                second_halo[ACROSS].start()
 
         def second_ions(x, carry):
             rows = rows_of(x)
@@ -466,15 +465,20 @@
             row = pl.ds(y, CX, stride=CY)
             out_ref[0, row] = base[1, row] + DT * diffusion_row(1, y)
         for side in (1, 0):
-            wait_side(second_halo, side)
+            second_halo[ACROSS_FIRST + side].wait_recv()
+            edges[1 - side].wait_recv()
+            second_halo[side].wait_send()
             finish_side(1, side, added)
             halo_rows(1)
             second_ions(ENDS[side], 0)
+            second_step((1, CX - 2)[side], 0)
+            if side == 0:
+                for copy in (*first_halo, *second_halo[2:], *edges, *tension):
+                    copy.wait_send()
+            wait_side(second_halo, side)
+            finish_far(side, added)
             second_step(ENDS[side], 0)
-            second_step((1, CX - 2)[side], 0)
             add_corners(1, side, added, second_halo)
-        for copy in (*first_halo, *second_halo[2:], *edges, *tension):
-            copy.wait_send()
 
 
     @pl.when(sec == 1)
@@ -485,16 +489,34 @@
         load_row = load(irow_ref, irow, 8)
         load_cls = load(cls_ref, cls, 9)
         load_ang = load(ang_ref, ang, 10)
-        load_u.start()
         load_ang.start()
         load_cls.start()
         load_row.start()
+        load_u.start()
         load_rest.start()
 
+        load_ang.wait()
+        load_cls.wait()
+        spread_fibers()
+
+        def take_list(values, slot):
+            source = jnp.broadcast_to(values.astype(F32), (CY, CY)).T
+            spot = lax.broadcasted_iota(jnp.int32, (CY, CY), 1).astype(F32)
+            rperm[slot] = jnp.where(source == spot, 1.0, 0.0).astype(BF16)
+
+        load_row.wait()
+        for side in range(2):
+            take_list(irow[side, 0], side)
+
+        def fiber_plane(x, carry):
+            for k, value in enumerate(fiber_of(x)):
+                fib[k, rows_of(x)] = value
+            return carry
+
+        lax.fori_loop(0, CX, fiber_plane, 0)
         load_u.wait()
         pack_rows(0, 3)
         load_rest.wait()
-        load_row.wait()
         pl.semaphore_wait(barrier, 3)
         first_halo = halo_copies(0, 3)
         stiff = (
@@ -511,25 +533,13 @@
             stiff[side].start()
             lists[side].start()
 
-        load_ang.wait()
-        load_cls.wait()
-        spread_fibers()
-
-        def take_list(values, slot):
-            source = jnp.broadcast_to(values.astype(F32), (CY, CY)).T
-            spot = lax.broadcasted_iota(jnp.int32, (CY, CY), 1).astype(F32)
-            rperm[slot] = jnp.where(source == spot, 1.0, 0.0).astype(BF16)
-
-        for side in range(2):
-            take_list(irow[side, 0], side)
-
         def weight_plane(x, carry):
             rows = rows_of(x)
             relax = 0.06 / inp[6, rows]
             rel[rows] = relax
             drive = relax * inp[7, rows]
-            for k, value in enumerate(fiber_of(x)):
-                fib[k, rows] = drive * value
+            for k in range(3):
+                fib[k, rows] = drive * fib[k, rows]
                 inp[3 + k, rows] = relax * inp[3 + k, rows]
             return carry
 
@@ -686,11 +696,11 @@
         )
         first_halo[ACROSS].wait_recv()
         halo_rows(0)
+        send_end(1, TEN_LAST)
+        send_end(0, TEN_FIRST)
         pack_edges(3)
         for copy in edges:
             copy.start()
-        send_end(1, TEN_LAST)
-        send_end(0, TEN_FIRST)
         receive(TEN_ROWS, trow)
         for side, y in ((0, CY - 1), (1, 0)):
             own = pl.ds(y, CX, stride=CY)
@@ -714,21 +724,22 @@
                 out_ref[k, own] = value + inp[3 + k, own] + fib[k, own] * trow[side]
         for side in (1, 0):
             x = ENDS[side]
-            second_halo[1 - side].wait_recv()
-            for k in range(3):
-                ext1[k, pl.ds((0, TOP)[side], CY)] += share[side, k]
             second_halo[ACROSS_FIRST + side].wait_recv()
             edges[1 - side].wait_recv()
             finish_side(3, side, added)
             halo_rows(1)
             last_plane((1, CX - 2)[side], 0)
+            shares[side].wait_recv()
+            if side == 0:
+                for copy in (*first_halo, *second_halo, *edges, *stiff, *lists, *shares):
+                    copy.wait_send()
+            second_halo[1 - side].wait_recv()
+            for k in range(3):
+                ext1[k, pl.ds((0, TOP)[side], CY)] += share[side, k]
             last_plane(x, 0)
             for k, value in enumerate(tie_forces(1, side)):
                 out_ref[k, rows_of(x)] += value
-            shares[side].wait_recv()
             add_corners(3, side, added, second_halo)
-        for copy in (*first_halo, *second_halo, *edges, *stiff, *lists, *shares):
-            copy.wait_send()
 
 
 def solution(mesh):

time: 22.9 us -> 22.7 us (level)
  no operation moved by 1% of the time
where the time goes in v5:
time: 22.7 us; the launch traced here: 22.6 us
  Pallas kernels  21.6 us (95%)
  local copies, waits for them, and re-layouts  0.97 us (4%)
    pallas_call x1, Pallas kernels, local(): pl.pallas_call(functools.partial(kernel, n_gx), out_shape=jax.ShapeDtypeS...  21.6 us
    unnamed x1, local copies, waits for them, and re-layouts  0.97 us

profile of v5, /device:TPU:1, one launch (start us, length us, event | category | flops | bytes accessed | tf_op | source)
XLA Modules:
  0.0 22.6 jit_solution(912625221695825541)
XLA Ops:
  0.0 21.6 %shard_map.55 = f32[4,512,128]{2,1,0:T(8,128)S(1)} custom-call(f32[8,512,128]{2,1,0:T(8,128)} %bitcast.7, f32[2,8]{1,0:T(2,128)} %bitcast.9, s32[128,32]{1,0:T(8,128)} %bitcast.8, s32[1,1,512]{2,1,0:T(1,128)} %rmap_ref.1, s32[2,1,1,32]{3,2,1,0:T(1,128)} %irow_ref.1), custom_call_target="tpu_custom_call" | custom-call | tf_op jit(solution)/shard_map/pallas_call | solution.py:751
  21.6 1.0 %copy.7 = f32[1,4,16,32,128]{4,3,2,1,0:T(8,128)} copy(f32[1,4,16,32,128]{4,3,2,1,0:T(8,128)S(1)} %bitcast.6) | data formatting | bytes 2097152

commit v6 on v5

--- a/solution.py
+++ b/solution.py
@@ -740,6 +740,17 @@
             for k, value in enumerate(tie_forces(1, side)):
                 out_ref[k, rows_of(x)] += value
             add_corners(3, side, added, second_halo)
+
+
+def deliver(from_ref, to_ref, sem):
+    copies = []
+    for k in range(8):
+        part = pl.ds(k % 2 * (COLS // 2), COLS // 2)
+        copies.append(pltpu.make_async_copy(from_ref.at[k // 2, part], to_ref.at[k // 2, part], sem.at[k]))
+    for copy in copies:
+        copy.start()
+    for copy in copies:
+        copy.wait()
 
 
 def solution(mesh):
@@ -794,6 +805,14 @@
         )(*[pltpu.with_memory_space_constraint(operand, pltpu.HBM) for operand in (
             sections.reshape(8, COLS, NZ), fiber_angles.T, fiber_class.transpose(0, 2, 1).reshape(CX * 8, CY), row_map,
             interface_rows)])
+        out = pl.pallas_call(
+            deliver,
+            out_shape=jax.ShapeDtypeStruct((4, COLS, NZ), F32),
+            in_specs=[pl.BlockSpec(memory_space=pltpu.VMEM)],
+            out_specs=pl.BlockSpec(memory_space=pl.ANY),
+            scratch_shapes=[pltpu.SemaphoreType.DMA((8,))],
+            compiler_params=pltpu.CompilerParams(vmem_limit_bytes=24 * 1024 * 1024),
+        )(pltpu.with_memory_space_constraint(out, pltpu.VMEM))
         return out.reshape(1, 4, CX, CY, NZ)
 
     in_specs = (

time: 22.7 us -> 22.8 us (level)
  Pallas kernels: 21.6 us -> 22.6 us
  local copies, waits for them, and re-layouts: 0.97 us -> 0 us
    pallas_call x0 -> x1, Pallas kernels: none -> 1.03 us  [local(): pl.pallas_call(deliver, out_shape=jax.ShapeDtypeStruct((4, COLS, NZ), F32...]
    unnamed x1 -> x0, local copies, waits for them, and re-layouts: 0.97 us -> none
where the time goes in v6:
time: 22.8 us; the launch traced here: 22.7 us
  Pallas kernels  22.6 us (99%)
    pallas_call x1, Pallas kernels, local(): pl.pallas_call(functools.partial(kernel, n_gx), out_shape=jax.ShapeDtypeS...  21.6 us
    pallas_call x1, Pallas kernels, local(): pl.pallas_call(deliver, out_shape=jax.ShapeDtypeStruct((4, COLS, NZ), F32...  1.03 us

profile of v6, /device:TPU:1, one launch (start us, length us, event | category | flops | bytes accessed | tf_op | source)
XLA Modules:
  0.0 22.7 jit_solution(1904602486552498501)
XLA Ops:
  0.0 21.6 %shard_map.55.from_ref = f32[4,512,128]{2,1,0:T(8,128)S(1)} custom-call(f32[8,512,128]{2,1,0:T(8,128)} %bitcast.6, f32[2,8]{1,0:T(2,128)} %bitcast.8, s32[128,32]{1,0:T(8,128)} %bitcast.7, s32[1,1,512]{2,1,0:T(1,128)} %rmap_ref.1, s32[2,1,1,32]{3,2,1,0:T(1,128)} %irow_ref.1), custom_call_target="tpu_custom_call" | custom-call | tf_op jit(solution)/shard_map/pallas_call | solution.py:762
  21.6 1.0 %shard_map.56 = f32[4,512,128]{2,1,0:T(8,128)} custom-call(f32[4,512,128]{2,1,0:T(8,128)S(1)} %shard_map.55.from_ref), custom_call_target="tpu_custom_call" | custom-call | tf_op jit(solution)/shard_map/pallas_call | solution.py:808
